TPU v7x, 32 devices: a whole 2x2x4 slice. The times are simulated.
32 devices in a mesh: row: 8 (over z, x), col: 4 (over y, core).
Axes of the slice: x: 2, y: 2, z: 4, core: 2. Of those that a mesh axis runs over, the one named last changes fastest.
Arguments:
- sources: float32 [128, 16384], P('col', 'row'), may hold values from -6 to 6
- tiles: bfloat16 [8, 4, 48, 256, 256], P('row', 'col')
- tile_row: int32 [8, 4, 48], P('row', 'col'), may hold values from 0 to 7
- tile_col: int32 [8, 4, 48], P('row', 'col'), may hold values from 0 to 15
- tile_count: int32 [8, 4], P('row', 'col'), may hold values from 1 to 48, as said below
Outputs:
- potential: float32 [128, 16384], P('col', 'row')
Inputs may be any that keep to these rules, and one draw needn't show every extreme that they name: `tile_count`: slots at or past a device's count hold no part of the operator; some device holds exactly 48 live slots; tile pairs may repeat and then add.
All inputs are finite; a program needn't handle non-finite values.
Results may differ from a plain program's by a relative error of at most 0.0029.
Values may be sent and summed in bfloat16 or wider, within the bound.
No kernel may reach another device: no remote copies, remote signals or barrier semaphores. Data moves between devices by JAX's collectives and lax.ppermute only.
A program may use at most 128 MiB of HBM per device.

v0:
```python
import math

import jax
import jax.numpy as jnp
import numpy as np
from jax import lax
from jax.sharding import PartitionSpec as P

ROOT_HALF = 1.0 / math.sqrt(2.0)
tile_group = 8


def swapped(value, axis, apart):
    mask = 2**apart
    pairs = [(source, source ^ mask) for source in range(lax.axis_size(axis))]
    return lax.ppermute(value, axis, pairs)


def haar_table(extent):
    matrix = np.eye(extent)
    stride = 1
    while stride < extent:
        for position in range(0, extent, 2 * stride):
            first_row = matrix[position].copy()
            second_row = matrix[position + stride].copy()
            matrix[position] = (first_row + second_row) * ROOT_HALF
            matrix[position + stride] = (first_row - second_row) * ROOT_HALF
        stride = stride * 2
    return matrix


def pair_step(values, stride):
    height, extent = values.shape
    shaped = values.reshape(height, extent // (2 * stride), 2, stride)
    first_part = shaped[:, :, 0, 0]
    second_part = shaped[:, :, 1, 0]
    shaped = shaped.at[:, :, 0, 0].set((first_part + second_part) * ROOT_HALF)
    shaped = shaped.at[:, :, 1, 0].set((first_part - second_part) * ROOT_HALF)
    return shaped.reshape(height, extent)


def haar_forward(values):
    stride = 1
    while stride < values.shape[1]:
        values = pair_step(values, stride)
        stride = stride * 2
    return values


def haar_inverse(values):
    stride = values.shape[1] // 2
    while stride >= 1:
        values = pair_step(values, stride)
        stride = stride // 2
    return values


def butterfly(coarse_value, partner, row_index, level_bit):
    active = row_index % 2**level_bit == 0
    upper_half = row_index // 2**level_bit % 2 == 1
    combined = jnp.where(upper_half, partner - coarse_value, partner + coarse_value) * ROOT_HALF
    return jnp.where(active, combined, coarse_value)


def forward_cross(coarse_value, row_index):
    bit_count = lax.axis_size("row").bit_length() - 1
    for level_bit in range(bit_count):
        partner = swapped(coarse_value, "row", level_bit)
        coarse_value = butterfly(coarse_value, partner, row_index, level_bit)
    return coarse_value


def inverse_cross(coarse_value, row_index):
    bit_count = lax.axis_size("row").bit_length() - 1
    for level_bit in reversed(range(bit_count)):
        partner = swapped(coarse_value, "row", level_bit)
        coarse_value = butterfly(coarse_value, partner, row_index, level_bit)
    return coarse_value


def local(sources, tiles, tile_row, tile_col, tile_count):
    extent = tiles.shape[-1]
    height = sources.shape[0]
    blocks = sources.shape[1] // extent
    haar_matrix = jnp.asarray(haar_table(extent), jnp.float32)
    row_index = lax.axis_index("row")
    col_index = lax.axis_index("col")
    shaped = sources.reshape(height, blocks, extent)
    local_coef = jnp.einsum("rbk,nk->rbn", shaped, haar_matrix, precision=lax.Precision.HIGHEST)
    scaling = haar_forward(local_coef[:, :, 0])
    first_value = scaling[:, 0:1]
    first_value = forward_cross(first_value, row_index)
    scaling = scaling.at[:, 0:1].set(first_value)
    wavelet = local_coef.at[:, :, 0].set(scaling).astype(jnp.bfloat16)
    all_sides = lax.all_gather(wavelet, "col", axis=0, tiled=True)
    owners = lax.axis_size("row") // lax.axis_size("col")
    group_blocks = blocks * owners
    every_block = lax.all_gather(all_sides, "row", axis=1, tiled=True)
    needed = lax.dynamic_slice_in_dim(every_block, col_index * group_blocks, group_blocks, 1)
    tile_stack = tiles.reshape(tiles.shape[2], extent, extent)
    rows_flat = tile_row.reshape(-1)
    cols_flat = tile_col.reshape(-1)
    live_count = tile_count.reshape(())
    groups = (live_count + tile_group - 1) // tile_group
    block_range = jnp.arange(blocks, dtype=jnp.int32)
    slot_range = jnp.arange(tile_group, dtype=jnp.int32)

    def accumulate(group_index, running):
        first_slot = group_index * tile_group
        group_tiles = lax.dynamic_slice_in_dim(tile_stack, first_slot, tile_group, 0)
        group_rows = lax.dynamic_slice_in_dim(rows_flat, first_slot, tile_group, 0)
        group_cols = lax.dynamic_slice_in_dim(cols_flat, first_slot, tile_group, 0)
        gathered_sides = jnp.take(needed, group_cols, axis=1)
        product = jnp.einsum(
            "rtk,tkn->rtn", gathered_sides, group_tiles, preferred_element_type=jnp.float32
        )
        usable = first_slot + slot_range < live_count
        select = ((group_rows[:, None] == block_range[None, :]) & usable[:, None]).astype(
            jnp.float32
        )
        return running + jnp.einsum("ti,rtn->rin", select, product, precision=lax.Precision.HIGHEST)

    image_coef = lax.psum_scatter(
        lax.fori_loop(
            0,
            groups,
            accumulate,
            jnp.zeros((height * lax.axis_size("col"), blocks, extent), jnp.float32),
        ),
        "col",
        scatter_dimension=0,
        tiled=True,
    )
    back_scaling = image_coef[:, :, 0]
    top_value = back_scaling[:, 0:1]
    top_value = inverse_cross(top_value, row_index)
    back_scaling = back_scaling.at[:, 0:1].set(top_value)
    back_scaling = haar_inverse(back_scaling)
    image_coef = image_coef.at[:, :, 0].set(back_scaling)
    result = jnp.einsum("rbn,nk->rbk", image_coef, haar_matrix, precision=lax.Precision.HIGHEST)
    return result.reshape(height, blocks * extent)


def solution(mesh):
    return jax.shard_map(
        local,
        mesh=mesh,
        in_specs=(
            P("col", "row"),
            P("row", "col", None, None, None),
            P("row", "col", None),
            P("row", "col", None),
            P("row", "col"),
        ),
        out_specs=P("col", "row"),
        check_vma=False,
    )
```

profile of v0, /device:TPU:0, one launch (start us, length us, event | category | flops | bytes accessed | tf_op | source)
XLA Modules:
  0.0 186.1 jit_solution(10615781243714369635)
XLA Ops:
  6.5 1.4 convolution_bitcast_fusion.2
  8.4 3.0 %collective-permute-start = (f32[32,1]{0,1:T(1,128)S(1)}, f32[32,1]{0,1:T(1,128)S(1)}, u32[]{:S(2)}, u32[]{:S(2)}) collective-permute-start(f32[32,1]{0,1:T(1,128)S(1)} %slice.458), channel_id=1, source_target_pairs={{0,4},{4,0},{8,12},{12,8},{16,20},{20,16},{24,28},{28,24},{1,5},{5... | collective-permute-start | bytes 392 | tf_op jit(solution)/shard_map/ppermute | solution.py:16
  11.3 1.5 collective-permute-done
  12.9 2.1 %collective-permute-start.1 = (f32[32,1]{0,1:T(1,128)S(1)}, f32[32,1]{0,1:T(1,128)S(1)}, u32[]{:S(2)}, u32[]{:S(2)}) collective-permute-start(f32[32,1]{0,1:T(1,128)S(1)} %fusion.23), channel_id=1, source_target_pairs={{0,8},{4,12},{8,0},{12,4},{16,24},{20,28},{24,16},{28,20},{1,9},{5... | collective-permute-start | bytes 392 | tf_op jit(solution)/shard_map/ppermute | solution.py:16
  15.0 1.5 collective-permute-done.1
  16.5 3.0 %collective-permute-start.2 = (f32[32,1]{0,1:T(1,128)S(1)}, f32[32,1]{0,1:T(1,128)S(1)}, u32[]{:S(2)}, u32[]{:S(2)}) collective-permute-start(f32[32,1]{0,1:T(1,128)S(1)} %broadcast_select_fusion.5), channel_id=1, source_target_pairs={{0,16},{4,20},{8,24},{12,28},{16,0},{20,4},{24,8},{28,12},{1,17},{... | collective-permute-start | bytes 392 | tf_op jit(solution)/shard_map/ppermute | solution.py:16
  21.9 8.0 %all_gather.6 = bf16[128,8,256]{2,0,1:T(8,128)(2,1)} all-gather(bf16[32,8,256]{2,0,1:T(8,128)(2,1)S(1)} %convert_element_type.5), channel_id=1, replica_groups=mesh['row'=8,'col'=4] {'col'}, dimensions={0}, use_global_device_ids=true | all-gather | bytes 655360 | tf_op jit(solution)/shard_map/all_gather | solution.py:95
  30.7 8.7 %copy.25 = bf16[1,1,48,256,256]{3,4,2,1,0:T(8,128)(2,1)} copy(bf16[1,1,48,256,256]{4,3,2,1,0:T(8,128)(2,1)} %param.41) | data formatting | bytes 12582912 | tf_op args[1]
  39.4 64.7 %all-gather.2.cloned.1.call-done = bf16[128,64,256]{2,0,1:T(8,128)(2,1)} async-done(((bf16[128,8,256]{2,0,1:T(8,128)(2,1)}), bf16[128,64,256]{2,0,1:T(8,128)(2,1)}) %all-gather.2.cloned.1.call-update) | async-done | bytes 4194320 | tf_op jit(solution)/shard_map/all_gather | solution.py:98
  104.1 2.3 %constant_dynamic-slice_fusion = bf16[128,16,256]{2,0,1:T(8,128)(2,1)} fusion(bf16[128,64,256]{2,0,1:T(8,128)(2,1)} %all-gather.2.cloned.1.call-done, s32[]{:T(128)S(6)} %select_n.142), kind=kLoop, calls=%fused_computation.59 | loop fusion | bytes 2097156 | tf_op jit(solution)/shard_map/dynamic_slice | solution.py:99
  106.5 5.7 %while.29 = (s32[]{:T(128)}, f32[128,8,256]{2,1,0:T(8,128)S(1)}, s32[]{:T(128)}, bf16[48,256,256]{1,2,0:T(8,128)(2,1)}, s32[48]{0:T(128)S(1)}, /*index=5*/bf16[1...) while((s32[]{:T(128)}, f32[128,8,256]{2,1,0:T(8,128)S(1)}, ...), condition=%wide.region_2.0_spmd.clone.clone, body=%wide.region_1.0_spmd.clone.clone.sunk | while | flops 159909056 | bytes 8917431 | solution.py:124
  107.4 1.8 gather_fusion
  109.2 1.7 convolution_bitcast_fusion.4
  112.2 1.0 copy-done
  113.2 48.6 %reduce-scatter.2.cloned.1.call-done = f32[32,8,256]{2,1,0:T(8,128)} async-done(((f32[128,8,256]{2,1,0:T(8,128)}), f32[32,8,256]{2,1,0:T(8,128)}) %reduce-scatter.2.cloned.1.call-update) | async-done | bytes 262160 | tf_op jit(solution)/shard_map/reduce_scatter | solution.py:123
  161.8 0.9 slice.477
  162.9 2.5 %collective-permute-start.3 = (f32[32,1]{0,1:T(1,128)S(1)}, f32[32,1]{0,1:T(1,128)S(1)}, u32[]{:S(2)}, u32[]{:S(2)}) collective-permute-start(f32[32,1]{0,1:T(1,128)S(1)} %slice.460), channel_id=1, source_target_pairs={{0,16},{4,20},{8,24},{12,28},{16,0},{20,4},{24,8},{28,12},{1,17},{... | collective-permute-start | bytes 392 | tf_op jit(solution)/shard_map/ppermute | solution.py:16
  165.3 2.0 %collective-permute-done.3 = f32[32,1]{0,1:T(1,128)S(1)} collective-permute-done((f32[32,1]{0,1:T(1,128)S(1)}, f32[32,1]{0,1:T(1,128)S(1)}, u32[]{:S(2)}, u32[]{:S(2)}) %collective-permute-start.3) | collective-permute-done | bytes 160 | tf_op jit(solution)/shard_map/ppermute | solution.py:16
  167.4 1.5 collective-permute-start.4
  168.9 2.0 %collective-permute-done.4 = f32[32,1]{0,1:T(1,128)S(1)} collective-permute-done((f32[32,1]{0,1:T(1,128)S(1)}, f32[32,1]{0,1:T(1,128)S(1)}, u32[]{:S(2)}, u32[]{:S(2)}) %collective-permute-start.4) | collective-permute-done | bytes 160 | tf_op jit(solution)/shard_map/ppermute | solution.py:16
  170.9 1.5 collective-permute-start.5
  172.4 1.2 slice_reduce_fusion.1
  175.5 1.6 scatter.79
  177.1 1.3 fusion.25
  (56 shorter events, 7.8 us)
Async XLA Ops:
  6.5 97.6 %all-gather.2.cloned.1.call-start = ((), (), s32[]{:S(2)}) async-start(), calls=%async_computation.1 | async-start | bytes 4718592 | tf_op jit(solution)/shard_map/all_gather | solution.py:98
  8.4 4.5 %collective-permute-start = (f32[32,1]{0,1:T(1,128)S(1)}, f32[32,1]{0,1:T(1,128)S(1)}, u32[]{:S(2)}, u32[]{:S(2)}) collective-permute-start(f32[32,1]{0,1:T(1,128)S(1)} %slice.458), channel_id=1, source_target_pairs={{0,4},{4,0},{8,12},{12,8},{16,20},{20,16},{24,28},{28,24},{1,5},{5... | collective-permute-start | bytes 392 | tf_op jit(solution)/shard_map/ppermute | solution.py:16
  12.9 3.6 %collective-permute-start.1 = (f32[32,1]{0,1:T(1,128)S(1)}, f32[32,1]{0,1:T(1,128)S(1)}, u32[]{:S(2)}, u32[]{:S(2)}) collective-permute-start(f32[32,1]{0,1:T(1,128)S(1)} %fusion.23), channel_id=1, source_target_pairs={{0,8},{4,12},{8,0},{12,4},{16,24},{20,28},{24,16},{28,20},{1,9},{5... | collective-permute-start | bytes 392 | tf_op jit(solution)/shard_map/ppermute | solution.py:16
  16.5 4.6 %collective-permute-start.2 = (f32[32,1]{0,1:T(1,128)S(1)}, f32[32,1]{0,1:T(1,128)S(1)}, u32[]{:S(2)}, u32[]{:S(2)}) collective-permute-start(f32[32,1]{0,1:T(1,128)S(1)} %broadcast_select_fusion.5), channel_id=1, source_target_pairs={{0,16},{4,20},{8,24},{12,28},{16,0},{20,4},{24,8},{28,12},{1,17},{... | collective-permute-start | bytes 392 | tf_op jit(solution)/shard_map/ppermute | solution.py:16
  30.0 131.9 %reduce-scatter.2.cloned.1.call-start = ((), (), s32[]{:S(2)}) async-start(), calls=%async_computation.2 | async-start | bytes 1310720 | tf_op jit(solution)/shard_map/reduce_scatter | solution.py:123
  30.7 75.8 %copy-start.2 = (s32[1,1,48]{2,1,0:T(1,128)S(1)}, s32[1,1,48]{2,1,0:T(1,128)}, u32[]{:S(2)}) copy-start(s32[1,1,48]{2,1,0:T(1,128)} %param.43) | copy-start | bytes 580
  30.7 75.8 %copy-start.3 = (s32[1,1,48]{2,1,0:T(1,128)S(1)}, s32[1,1,48]{2,1,0:T(1,128)}, u32[]{:S(2)}) copy-start(s32[1,1,48]{2,1,0:T(1,128)} %param.42) | copy-start | bytes 580
  106.5 70.6 %copy-start.1 = (f32[256,256,1]{1,0,2:T(8,128)S(1)}, f32[256,256,1]{1,0,2:T(8,128)}, u32[]{:S(2)}) copy-start(f32[256,256,1]{1,0,2:T(8,128)} %constant.538) | copy-start | bytes 786436
  112.2 1.0 copy-start
  162.9 4.5 %collective-permute-start.3 = (f32[32,1]{0,1:T(1,128)S(1)}, f32[32,1]{0,1:T(1,128)S(1)}, u32[]{:S(2)}, u32[]{:S(2)}) collective-permute-start(f32[32,1]{0,1:T(1,128)S(1)} %slice.460), channel_id=1, source_target_pairs={{0,16},{4,20},{8,24},{12,28},{16,0},{20,4},{24,8},{28,12},{1,17},{... | collective-permute-start | bytes 392 | tf_op jit(solution)/shard_map/ppermute | solution.py:16
  167.4 3.5 %collective-permute-start.4 = (f32[32,1]{0,1:T(1,128)S(1)}, f32[32,1]{0,1:T(1,128)S(1)}, u32[]{:S(2)}, u32[]{:S(2)}) collective-permute-start(f32[32,1]{0,1:T(1,128)S(1)} %broadcast_select_fusion.8), channel_id=1, source_target_pairs={{0,8},{4,12},{8,0},{12,4},{16,24},{20,28},{24,16},{28,20},{1,9},{5... | collective-permute-start | bytes 392 | tf_op jit(solution)/shard_map/ppermute | solution.py:16
  170.9 3.5 %collective-permute-start.5 = (f32[32,1]{0,1:T(1,128)S(1)}, f32[32,1]{0,1:T(1,128)S(1)}, u32[]{:S(2)}, u32[]{:S(2)}) collective-permute-start(f32[32,1]{0,1:T(1,128)S(1)} %broadcast_select_fusion.4), channel_id=1, source_target_pairs={{0,4},{4,0},{8,12},{12,8},{16,20},{20,16},{24,28},{28,24},{1,5},{5... | collective-permute-start | bytes 392 | tf_op jit(solution)/shard_map/ppermute | solution.py:16
Sparse Core Ops, SparseCore 0:
  30.1 73.9 all-gather.1
  113.3 48.4 reduce-scatter.1
where the time goes:
time: 188 us; the launch traced here: 186 us
  waiting for transfers between devices  122 us (65%)
  local copies, waits for them, and re-layouts  20.1 us (11%)
  between operations  14.2 us (8%)
  starting transfers between devices  13.6 us (7%)
  blocking collectives  8 us (4%)
  matrix products  5.33 us (3%)
  other arithmetic  2.76 us (1%)
    all_gather x1, waiting for transfers between devices, local(): every_block = lax.all_gather(all_sides, 'row', axis=1, tiled=True)  64.7 us
    reduce_scatter x1, waiting for transfers between devices, local(): lax.psum_scatter(lax.fori_loop(0, groups, accumulate, jnp.zeros((height *...  48.6 us
    ppermute x6, starting transfers between devices, swapped(): return lax.ppermute(value, axis, pairs)  13.5 us
    unnamed x11, local copies, waits for them, and re-layouts  10.6 us
    ppermute x6, waiting for transfers between devices, swapped(): return lax.ppermute(value, axis, pairs)  8.66 us
    all_gather x1, blocking collectives, local(): all_sides = lax.all_gather(wavelet, 'col', axis=0, tiled=True)  8 us
  transfers between devices with their start and end apart: 8, of which 8 were waited for; matrix products, arithmetic and copies ran while one was open for 6% of the time, Pallas kernels for 0%

commit v1 on v0

v1 whole, which is shorter than its diff:
```python
import functools
import math

import jax
import jax.numpy as jnp
import numpy as np
from jax import lax
from jax.experimental import pallas as pl
from jax.experimental.pallas import tpu as pltpu
from jax.sharding import PartitionSpec as P

ROOT_HALF = 1.0 / math.sqrt(2.0)
SIDE_ROWS = 16
SLOT_GROUP = 8
MIB = 2**20


def haar_table(extent):
    matrix = np.eye(extent)
    stride = 1
    while stride < extent:
        for position in range(0, extent, 2 * stride):
            first_row = matrix[position].copy()
            second_row = matrix[position + stride].copy()
            matrix[position] = (first_row + second_row) * ROOT_HALF
            matrix[position + stride] = (first_row - second_row) * ROOT_HALF
        stride = stride * 2
    return matrix


def haar_parts(extent):
    matrix = haar_table(extent)
    scale = np.max(np.abs(matrix), axis=1)
    signs = np.round(matrix / scale[:, None])
    return signs.T, scale[None, :]


def three_terms(value):
    high = value.astype(jnp.bfloat16)
    rest = value - high.astype(jnp.float32)
    middle = rest.astype(jnp.bfloat16)
    low = (rest - middle.astype(jnp.float32)).astype(jnp.bfloat16)
    return high, middle, low


def exact_dot(value, signs):
    return sum(jnp.dot(term, signs, preferred_element_type=jnp.float32) for term in three_terms(value))


def block_forward(columns):
    columns = list(columns)
    stride = 1
    while stride < len(columns):
        for p in range(0, len(columns), 2 * stride):
            u, v = columns[p], columns[p + stride]
            columns[p], columns[p + stride] = (u + v) * ROOT_HALF, (u - v) * ROOT_HALF
        stride *= 2
    return columns


def block_inverse(columns):
    columns = list(columns)
    stride = len(columns) // 2
    while stride >= 1:
        for p in range(0, len(columns), 2 * stride):
            u, v = columns[p], columns[p + stride]
            columns[p], columns[p + stride] = (u + v) * ROOT_HALF, (u - v) * ROOT_HALF
        stride //= 2
    return columns


def front_kernel(core_ref, mine_ref, other_ref, signs_ref, scale_ref, out_ref, *, blocks, extent):
    height = mine_ref.shape[0]
    pair = 2 * height
    mine, other = mine_ref[...], other_ref[...]
    first_core = core_ref[0] == 0
    both = jnp.concatenate([jnp.where(first_core, mine, other), jnp.where(first_core, other, mine)], axis=0)
    parts = [both[:, b * extent : (b + 1) * extent] for b in range(blocks)]
    coef = exact_dot(jnp.concatenate(parts, axis=0), signs_ref[...]) * scale_ref[...]
    columns = block_forward([coef[b * pair : (b + 1) * pair, 0:1] for b in range(blocks)])
    lane = lax.broadcasted_iota(jnp.int32, (pair, extent), 1)
    for b in range(blocks):
        column = jnp.zeros_like(columns[0]) if b == 0 else columns[b]
        block = jnp.where(lane == 0, column, coef[b * pair : (b + 1) * pair, :])
        out_ref[b * pair : (b + 1) * pair, :] = block.astype(jnp.bfloat16)
    total = functools.reduce(jnp.add, parts)
    ones = jnp.ones((SIDE_ROWS, extent), jnp.bfloat16)
    first = sum(
        lax.dot_general(ones, term, (((1,), (1,)), ((), ())), preferred_element_type=jnp.float32)
        for term in three_terms(total)
    ) * (1.0 / math.sqrt(blocks * extent))
    high, middle, low = (term.astype(jnp.float32) for term in three_terms(first))
    row = lax.broadcasted_iota(jnp.int32, first.shape, 0)
    side = jnp.where(row == 0, high, jnp.where(row == 1, middle, jnp.where(row == 2, low, 0.0)))
    out_ref[blocks * pair :, :] = jnp.zeros((SIDE_ROWS, extent), jnp.bfloat16)
    out_ref[blocks * pair :, 0:pair] = side.astype(jnp.bfloat16)


def edge_kernel(rows_ref, cols_ref, count_ref, tiles_ref, first_cols_ref, first_row_ref, *, blocks):
    step = pl.program_id(0)
    extent = tiles_ref.shape[-1]

    @pl.when(step == 0)
    def _():
        first_cols_ref[...] = jnp.zeros_like(first_cols_ref)
        first_row_ref[...] = jnp.zeros_like(first_row_ref)

    pick = (lax.broadcasted_iota(jnp.int32, (SIDE_ROWS, extent), 1) == 0).astype(jnp.bfloat16)
    for s in range(SLOT_GROUP):
        slot = step * SLOT_GROUP + s
        live = slot < count_ref[0]
        row, col = rows_ref[slot], cols_ref[slot]

        @pl.when(live & (lax.rem(col, blocks) == 0))
        def _():
            at = pl.ds(col + row, 1)
            first_cols_ref[at, :] += tiles_ref[s, 0:SIDE_ROWS, :].astype(jnp.float32)[0:1, :]

        @pl.when(live & (row == 0))
        def _():
            column = lax.dot_general(
                pick, tiles_ref[s], (((1,), (1,)), ((), ())), preferred_element_type=jnp.float32
            )
            first_row_ref[pl.ds(col, 1), :] += column[0:1, :]


def product_kernel(
    rows_ref, cols_ref, count_ref, place_ref, tiles_ref, first_cols_ref, first_row_ref, *refs, blocks, owners, spans
):
    messages = refs[: owners * spans]
    keep_ref, send_ref, sides, acc, firsts = refs[owners * spans :]
    step = pl.program_id(0)
    extent = tiles_ref.shape[-1]
    pair = sides.shape[1] // spans
    height = pair // 2

    @pl.when(step == 0)
    def _():
        for index, message in enumerate(messages):
            owner, at = place_ref[2 * index + 1], place_ref[2 * index + 2]
            rows = pl.ds(pl.multiple_of(at * pair, pair), pair)
            for b in range(blocks):
                sides[owner * blocks + b, rows, :] = message[b * pair : (b + 1) * pair, :]
            side = jnp.transpose(message[blocks * pair :, :].astype(jnp.float32))
            column = side[0:pair, 0:1] + side[0:pair, 1:2] + side[0:pair, 2:3]
            firsts[owner, rows, :] = jnp.broadcast_to(column, (pair, firsts.shape[2]))
        lane = lax.broadcasted_iota(jnp.int32, (1, extent), 1)
        for i in range(blocks):
            total = jnp.zeros(acc.shape[1:], jnp.float32)
            for owner in range(owners):
                line = first_cols_ref[owner * blocks + i : owner * blocks + i + 1, :]
                if i == 0:
                    line = jnp.where(lane == 0, 0.0, line)
                total += firsts[owner][:, 0:1] * line
            acc[i] = total

    count = count_ref[0]
    for s in range(SLOT_GROUP):
        slot = step * SLOT_GROUP + s

        @pl.when(slot < count)
        def _():
            row, col = rows_ref[slot], cols_ref[slot]
            acc[row] += jnp.dot(sides[col], tiles_ref[s], preferred_element_type=jnp.float32)

    @pl.when(step == pl.num_programs(0) - 1)
    def _():
        total = jnp.zeros(acc.shape[1:], jnp.float32)
        for b in range(blocks * owners):
            total += sides[b].astype(jnp.float32) * first_row_ref[b : b + 1, :]
        top = jnp.sum(total, axis=1, keepdims=True)
        for owner in range(owners):
            top += firsts[owner][:, 0:1] * first_row_ref[owner * blocks : owner * blocks + 1, 0:1]
        lane = lax.broadcasted_iota(jnp.int32, acc.shape[1:], 1)
        acc[0] = jnp.where(lane == 0, top, acc[0])
        first_core = place_ref[0] == 0
        for i in range(blocks):
            value = acc[i]
            for y in range(spans):
                one = value[y * pair : y * pair + height, :]
                two = value[y * pair + height : (y + 1) * pair, :]
                keep_ref[y, i] = jnp.where(first_core, one, two)
                send_ref[y, i] = jnp.where(first_core, two, one)


def combine_kernel(span_ref, keep_ref, arrived_ref, own_ref, *out_refs):
    spans = keep_ref.shape[0]
    span = span_ref[0]
    own_ref[...] = keep_ref[span] + arrived_ref[span]
    for j, out_ref in enumerate(out_refs, 1):
        at = lax.rem(span + j, spans)
        out_ref[...] = (keep_ref[at] + arrived_ref[at]).astype(jnp.bfloat16)


def back_kernel(own_ref, *refs):
    *arrived, signs_ref, scale_ref, out_ref = refs
    blocks, height, extent = own_ref.shape
    total = own_ref[...]
    for part in arrived:
        total = total + part[...].astype(jnp.float32)
    columns = block_inverse([total[b][:, 0:1] for b in range(blocks)])
    lane = lax.broadcasted_iota(jnp.int32, (height, extent), 1)
    fixed = jnp.concatenate([jnp.where(lane == 0, columns[b], total[b]) for b in range(blocks)], axis=0)
    result = exact_dot(fixed * scale_ref[...], signs_ref[...])
    for b in range(blocks):
        out_ref[:, b * extent : (b + 1) * extent] = result[b * height : (b + 1) * height, :]


def butterfly(value, partner, index, bit):
    active = index % 2**bit == 0
    upper = index // 2**bit % 2 == 1
    combined = jnp.where(upper, partner - value, partner + value) * ROOT_HALF
    return jnp.where(active, combined, value)


def inverse_cross(value, axis):
    size = lax.axis_size(axis)
    index = lax.axis_index(axis)
    for bit in reversed(range(size.bit_length() - 1)):
        pairs = [(source, source ^ 2**bit) for source in range(size)]
        value = butterfly(value, lax.ppermute(value, axis, pairs), index, bit)
    return value


def local(sources, tiles, tile_row, tile_col, tile_count):
    n_row, n_col = lax.axis_size("row"), lax.axis_size("col")
    owners = n_row // n_col
    spans = n_col // 2
    extent = tiles.shape[-1]
    slots = tiles.shape[2]
    height = sources.shape[0]
    blocks = sources.shape[1] // extent
    pair = 2 * height
    row_index, col_index = lax.axis_index("row"), lax.axis_index("col")
    z, x = row_index // owners, row_index % owners
    span, core = col_index // 2, col_index % 2
    signs, scale = haar_parts(extent)

    def moved(value, to):
        pairs = []
        for a in range(n_row):
            for b in range(n_col):
                zz, xx, yy, cc = to(a // owners, a % owners, b // 2, b % 2)
                pairs.append((a * n_col + b, (zz * owners + xx) * n_col + yy * 2 + cc))
        return lax.ppermute(value, ("row", "col"), pairs)

    def other_core(value):
        return moved(value, lambda zz, xx, yy, cc: (zz, xx, yy, 1 - cc))

    smem = pl.BlockSpec(memory_space=pltpu.SMEM)
    vmem = pl.BlockSpec(memory_space=pltpu.VMEM)

    message = pl.pallas_call(
        functools.partial(front_kernel, blocks=blocks, extent=extent),
        out_shape=jax.ShapeDtypeStruct((blocks * pair + SIDE_ROWS, extent), jnp.bfloat16),
        in_specs=[smem, vmem, vmem, vmem, vmem],
        out_specs=vmem,
        name="front",
        compiler_params=pltpu.CompilerParams(vmem_limit_bytes=16 * MIB),
        cost_estimate=pl.CostEstimate(flops=6 * blocks * pair * extent * extent, bytes_accessed=MIB, transcendentals=0),
    )(
        core.astype(jnp.int32).reshape(1),
        sources,
        other_core(sources),
        jnp.asarray(signs, jnp.bfloat16),
        jnp.asarray(scale, jnp.float32),
    )

    pieces, places = [], [core]
    direct = [
        moved(message, lambda zz, xx, yy, cc, m=m: (cc * spans + (yy + m) % spans, xx, zz // 2, zz % 2))
        for m in range(spans)
    ]
    for m in range(spans):
        came_from = (z % spans - m) % spans
        pieces.append(direct[m])
        places += [x, came_from]
        for j in range(1, owners):
            pieces.append(moved(direct[m], lambda zz, xx, yy, cc, j=j: (zz, (xx + j) % owners, yy, cc)))
            places += [(x - j) % owners, came_from]

    stack = tiles.reshape(slots, extent, extent)
    rows_flat, cols_flat = tile_row.reshape(-1), tile_col.reshape(-1)
    count = tile_count.reshape(1)
    steps = slots // SLOT_GROUP

    def tile_block(step, rows_ref, cols_ref, count_ref, *_):
        return jnp.minimum(step, (count_ref[0] - 1) // SLOT_GROUP), 0, 0

    first_cols, first_row = pl.pallas_call(
        functools.partial(edge_kernel, blocks=blocks),
        out_shape=[
            jax.ShapeDtypeStruct((owners * blocks, extent), jnp.float32),
            jax.ShapeDtypeStruct((owners * blocks, extent), jnp.float32),
        ],
        grid_spec=pltpu.PrefetchScalarGridSpec(
            num_scalar_prefetch=3,
            grid=(steps,),
            in_specs=[pl.BlockSpec((SLOT_GROUP, extent, extent), tile_block)],
            out_specs=[pl.BlockSpec((owners * blocks, extent), lambda *_: (0, 0))] * 2,
        ),
        name="edges",
        compiler_params=pltpu.CompilerParams(vmem_limit_bytes=16 * MIB),
        cost_estimate=pl.CostEstimate(flops=0, bytes_accessed=stack.size * 2, transcendentals=0),
    )(rows_flat, cols_flat, count, stack)

    by_owner = first_cols.reshape(owners, blocks, extent)
    by_owner = block_inverse([inverse_cross(by_owner[0], "col")] + [by_owner[i] for i in range(1, owners)])
    first_cols = jnp.concatenate(by_owner, axis=0)
    corner = jnp.stack([part[0, 0] for part in by_owner])
    first_row = inverse_cross(first_row.at[::blocks, 0].set(corner), "row")

    shape = (spans, blocks, height, extent)
    whole = lambda *dims: pl.BlockSpec(dims, lambda *_: (0,) * len(dims))
    keep, send = pl.pallas_call(
        functools.partial(product_kernel, blocks=blocks, owners=owners, spans=spans),
        out_shape=[jax.ShapeDtypeStruct(shape, jnp.float32)] * 2,
        grid_spec=pltpu.PrefetchScalarGridSpec(
            num_scalar_prefetch=4,
            grid=(steps,),
            in_specs=[
                pl.BlockSpec((SLOT_GROUP, extent, extent), tile_block),
                whole(owners * blocks, extent),
                whole(owners * blocks, extent),
            ]
            + [whole(blocks * pair + SIDE_ROWS, extent)] * (owners * spans),
            out_specs=[whole(*shape)] * 2,
            scratch_shapes=[
                pltpu.VMEM((owners * blocks, spans * pair, extent), jnp.bfloat16),
                pltpu.VMEM((blocks, spans * pair, extent), jnp.float32),
                pltpu.VMEM((owners, spans * pair, 128), jnp.float32),
            ],
        ),
        name="products",
        compiler_params=pltpu.CompilerParams(vmem_limit_bytes=32 * MIB),
        cost_estimate=pl.CostEstimate(
            flops=2 * slots * spans * pair * extent * extent, bytes_accessed=stack.size * 2, transcendentals=0
        ),
    )(rows_flat, cols_flat, count, jnp.stack(places).astype(jnp.int32), stack, first_cols, first_row, *pieces)

    part = jax.ShapeDtypeStruct(shape[1:], jnp.bfloat16)
    own, *outgoing = pl.pallas_call(
        combine_kernel,
        out_shape=[jax.ShapeDtypeStruct(shape[1:], jnp.float32)] + [part] * (spans - 1),
        in_specs=[smem, vmem, vmem],
        out_specs=[vmem] * spans,
        name="combine",
        compiler_params=pltpu.CompilerParams(vmem_limit_bytes=16 * MIB),
    )(span.astype(jnp.int32).reshape(1), keep, other_core(send))
    arrived = [
        moved(value, lambda zz, xx, yy, cc, j=j: (zz, xx, (yy + j) % spans, cc)) for j, value in enumerate(outgoing, 1)
    ]
    return pl.pallas_call(
        back_kernel,
        out_shape=jax.ShapeDtypeStruct(sources.shape, jnp.float32),
        in_specs=[vmem] * (spans + 2),
        out_specs=vmem,
        name="back",
        compiler_params=pltpu.CompilerParams(vmem_limit_bytes=16 * MIB),
    )(own, *arrived, jnp.asarray(signs.T, jnp.bfloat16), jnp.asarray(scale, jnp.float32))


def solution(mesh):
    return jax.shard_map(
        local,
        mesh=mesh,
        in_specs=(
            P("col", "row"),
            P("row", "col", None, None, None),
            P("row", "col", None),
            P("row", "col", None),
            P("row", "col"),
        ),
        out_specs=P("col", "row"),
        check_vma=False,
    )
```

time: 188 us -> 66.4 us (0.35)
  the two profiles are of different devices: /device:TPU:0 before, /device:TPU:8 now
where the time goes in v1:
time: 66.4 us; the launch traced here: 65.7 us
  waiting for transfers between devices  29.2 us (44%)
  starting transfers between devices  14.6 us (22%)
  Pallas kernels  10.8 us (16%)
  local copies, waits for them, and re-layouts  8.72 us (13%)
  other arithmetic  1.36 us (2%)
  between operations  0.95 us (1%)
    ppermute x7, waiting for transfers between devices, moved(): return lax.ppermute(value, ('row', 'col'), pairs)  20.1 us
    ppermute x5, waiting for transfers between devices, inverse_cross(): value = butterfly(value, lax.ppermute(value, axis, pairs), index, bit)  9.13 us
    ppermute x7, starting transfers between devices, moved(): return lax.ppermute(value, ('row', 'col'), pairs)  8.41 us
    pallas_call x1, Pallas kernels, local(): pl.pallas_call(functools.partial(product_kernel, blocks=blocks, owners=ow...  7.32 us
    unnamed x20, local copies, waits for them, and re-layouts  6.9 us
    ppermute x5, starting transfers between devices, inverse_cross(): value = butterfly(value, lax.ppermute(value, axis, pairs), index, bit)  6.24 us
    pallas_call x1, Pallas kernels, local(): pl.pallas_call(functools.partial(edge_kernel, blocks=blocks), out_shape=[...  1.85 us
  transfers between devices with their start and end apart: 12, of which 7 were waited for; matrix products, arithmetic and copies ran while one was open for 5% of the time, Pallas kernels for 1%

profile of v1, /device:TPU:8, one launch (start us, length us, event | category | flops | bytes accessed | tf_op | source)
XLA Modules:
  0.0 65.7 jit_solution(11746805606426927051)
XLA Ops:
  0.7 2.8 %copy-done = bf16[1,1,48,256,256]{4,3,2,1,0:T(8,128)(2,1)S(1)} copy-done((bf16[1,1,48,256,256]{4,3,2,1,0:T(8,128)(2,1)S(1)}, bf16[1,1,48,256,256]{4,3,2,1,0:T(8,128)(2,1)}, u32[]{:S(2)}) %copy-start) | copy-done | bytes 6291480
  3.5 0.7 copy-done.6
  4.1 0.7 copy-done.8
  4.8 1.9 %edges.1 = (f32[16,256]{1,0:T(8,128)S(1)}, f32[16,256]{1,0:T(8,128)S(1)}) custom-call(s32[48]{0:T(128)S(1)} %bitcast.19, s32[48]{0:T(128)S(1)} %bitcast.21, s32[1]{0:T(128)} %bitcast.14.count_ref, bf16[48,256,256]{2,1,0:T(8,128)(2,1)S(1)} %bitcast.17), custom_call_target="tpu_custom_call" | custom-call | bytes 6291456 | tf_op jit(solution)/shard_map/edges/pallas_call | solution.py:290
  6.7 1.4 %collective-permute-start = (f32[8,256]{1,0:T(8,128)S(1)}, f32[8,256]{1,0:T(8,128)S(1)}, u32[]{:S(2)}, u32[]{:S(2)}) collective-permute-start(f32[8,256]{1,0:T(8,128)S(1)} %slice.14), channel_id=1, source_target_pairs={{0,2},{1,3},{2,0},{3,1},{4,6},{5,7},{6,4},{7,5},{8,10},{9,11},{10,... | collective-permute-start | bytes 24584 | tf_op jit(solution)/shard_map/ppermute | solution.py:221
  8.1 2.3 %collective-permute-done = f32[8,256]{1,0:T(8,128)S(1)} collective-permute-done((f32[8,256]{1,0:T(8,128)S(1)}, f32[8,256]{1,0:T(8,128)S(1)}, u32[]{:S(2)}, u32[]{:S(2)}) %collective-permute-start) | collective-permute-done | bytes 8224 | tf_op jit(solution)/shard_map/ppermute | solution.py:221
  10.5 1.1 %collective-permute-done.1 = f32[8,256]{1,0:T(8,128)S(1)} collective-permute-done((f32[8,256]{1,0:T(8,128)S(1)}, f32[8,256]{1,0:T(8,128)S(1)}, u32[]{:S(2)}, u32[]{:S(2)}) %collective-permute-start.1) | collective-permute-done | bytes 8224 | tf_op jit(solution)/shard_map/ppermute | solution.py:221
  11.6 0.5 slice.21
  12.1 0.6 slice.20
  12.7 1.3 %pad_maximum_fusion.1 = f32[2]{0:T(128)S(1)} fusion(f32[1]{0:T(128)} %bitcast.12, f32[1]{0:T(128)} %bitcast.11), kind=kLoop, calls=%fused_computation.12 | loop fusion | flops 2 | bytes 16 | tf_op jit(solution)/shard_map/stack | solution.py:310
  14.0 0.6 scatter_fusion
  14.6 2.4 %collective-permute-start.2 = (f32[16,256]{1,0:T(8,128)S(1)}, f32[16,256]{1,0:T(8,128)S(1)}, u32[]{:S(2)}, u32[]{:S(2)}) collective-permute-start(f32[16,256]{1,0:T(8,128)S(1)} %scatter_fusion), channel_id=1, source_target_pairs={{0,16},{4,20},{8,24},{12,28},{16,0},{20,4},{24,8},{28,12},{1,17},{... | collective-permute-start | bytes 49160 | tf_op jit(solution)/shard_map/ppermute | solution.py:221
  17.6 3.6 %collective-permute-start.6 = (bf16[528,256]{1,0:T(8,128)(2,1)S(1)}, bf16[528,256]{1,0:T(8,128)(2,1)S(1)}, u32[]{:S(2)}, u32[]{:S(2)}) collective-permute-start(bf16[528,256]{1,0:T(8,128)(2,1)S(1)} %front.1), channel_id=1, source_target_pairs={{0,0},{1,16},{2,8},{3,24},{4,4},{5,20},{6,12},{7,28},{8,1},{9,17},... | collective-permute-start | bytes 811016 | tf_op jit(solution)/shard_map/ppermute | solution.py:245
  21.5 5.7 %collective-permute-done.3 = f32[16,256]{1,0:T(8,128)S(1)} collective-permute-done((f32[16,256]{1,0:T(8,128)S(1)}, f32[16,256]{1,0:T(8,128)S(1)}, u32[]{:S(2)}, u32[]{:S(2)}) %collective-permute-start.3) | collective-permute-done | bytes 16416 | tf_op jit(solution)/shard_map/ppermute | solution.py:221
  27.3 2.3 %collective-permute-start.4 = (f32[16,256]{1,0:T(8,128)S(1)}, f32[16,256]{1,0:T(8,128)S(1)}, u32[]{:S(2)}, u32[]{:S(2)}) collective-permute-start(f32[16,256]{1,0:T(8,128)S(1)} %multiply_select_fusion), channel_id=1, source_target_pairs={{0,4},{4,0},{8,12},{12,8},{16,20},{20,16},{24,28},{28,24},{1,5},{5... | collective-permute-start | bytes 49160 | tf_op jit(solution)/shard_map/ppermute | solution.py:221
  29.7 1.9 %collective-permute-start.7 = (bf16[528,256]{1,0:T(8,128)(2,1)S(1)}, bf16[528,256]{1,0:T(8,128)(2,1)S(1)}, u32[]{:S(2)}, u32[]{:S(2)}) collective-permute-start(bf16[528,256]{1,0:T(8,128)(2,1)S(1)} %collective-permute-done.6.refs_0_), channel_id=1, source_target_pairs={{0,4},{1,5},{2,6},{3,7},{4,0},{5,1},{6,2},{7,3},{8,12},{9,13},{10,... | collective-permute-start | bytes 811016 | tf_op jit(solution)/shard_map/ppermute | solution.py:245
  31.7 7.0 %collective-permute-done.9.refs_3_ = bf16[528,256]{1,0:T(8,128)(2,1)S(1)} collective-permute-done((bf16[528,256]{1,0:T(8,128)(2,1)S(1)}, bf16[528,256]{1,0:T(8,128)(2,1)S(1)}, u32[]{:S(2)}, u32[]{:S(2)}) %collective-permute-start.9) | collective-permute-done | bytes 270368 | tf_op jit(solution)/shard_map/ppermute | solution.py:245
  38.7 5.8 %collective-permute-done.7.refs_1_ = bf16[528,256]{1,0:T(8,128)(2,1)S(1)} collective-permute-done((bf16[528,256]{1,0:T(8,128)(2,1)S(1)}, bf16[528,256]{1,0:T(8,128)(2,1)S(1)}, u32[]{:S(2)}, u32[]{:S(2)}) %collective-permute-start.7) | collective-permute-done | bytes 270368 | tf_op jit(solution)/shard_map/ppermute | solution.py:245
  44.5 2.8 %copy-done.1 = bf16[1,1,48,256,256]{4,3,2,1,0:T(8,128)(2,1)S(1)} copy-done((bf16[1,1,48,256,256]{4,3,2,1,0:T(8,128)(2,1)S(1)}, bf16[1,1,48,256,256]{4,3,2,1,0:T(8,128)(2,1)}, u32[]{:S(2)}) %copy-start.1) | copy-done | bytes 6291480
  47.3 7.3 %products.1 = (f32[2,8,32,256]{3,2,1,0:T(8,128)S(1)}, f32[2,8,32,256]{3,2,1,0:T(8,128)S(1)}) custom-call(s32[48]{0:T(128)S(1)} %bitcast.20, s32[48]{0:T(128)S(1)} %bitcast.22, s32[1]{0:T(128)} %bitcast.15.count_ref, s32[9]{0:T(128)S(1)} %stack.30.place_ref, bf16[48,256,256]{2,1,0:T(8,128)(2,1)S(1)} %bitcast.18, ...), custom_call_target="tpu_custom_call" | custom-call | flops 805306368 | bytes 6291456 | tf_op jit(solution)/shard_map/products/pallas_call | solution.py:315
  54.6 2.6 %collective-permute-start.10 = (f32[2,8,32,256]{3,2,1,0:T(8,128)S(1)}, f32[2,8,32,256]{3,2,1,0:T(8,128)S(1)}, u32[]{:S(2)}, u32[]{:S(2)}) collective-permute-start(f32[2,8,32,256]{3,2,1,0:T(8,128)S(1)} %get-tuple-element.14), channel_id=1, source_target_pairs={{0,1},{1,0},{2,3},{3,2},{4,5},{5,4},{6,7},{7,6},{8,9},{9,8},{10,11... | collective-permute-start | bytes 1572872 | tf_op jit(solution)/shard_map/ppermute | solution.py:245
  57.2 1.5 %collective-permute-done.10.arrived_ref = f32[2,8,32,256]{3,2,1,0:T(8,128)S(1)} collective-permute-done((f32[2,8,32,256]{3,2,1,0:T(8,128)S(1)}, f32[2,8,32,256]{3,2,1,0:T(8,128)S(1)}, u32[]{:S(2)}, u32[]{:S(2)}) %collective-permute-start.10) | collective-permute-done | bytes 524320 | tf_op jit(solution)/shard_map/ppermute | solution.py:245
  58.9 5.8 %collective-permute-done.11.refs_0_ = bf16[8,32,256]{2,1,0:T(8,128)(2,1)S(1)} collective-permute-done((bf16[8,32,256]{2,1,0:T(8,128)(2,1)S(1)}, bf16[8,32,256]{2,1,0:T(8,128)(2,1)S(1)}, u32[]{:S(2)}, u32[]{:S(2)}) %collective-permute-start.11) | collective-permute-done | bytes 131104 | tf_op jit(solution)/shard_map/ppermute | solution.py:245
  64.7 1.0 %back.1 = f32[32,2048]{1,0:T(8,128)} custom-call(f32[8,32,256]{2,1,0:T(8,128)S(1)} %get-tuple-element.15.own_ref, bf16[8,32,256]{2,1,0:T(8,128)(2,1)S(1)} %collective-permute-done.11.refs_0_, bf16[256,256]{1,0:T(8,128)(2,1)S(1)} %copy-done.3, f32[1,256]{1,0:T(1,128)S(1)} %copy-done.5), custom_call_target="tpu_custom_call" | custom-call | tf_op jit(solution)/shard_map/back/pallas_call | solution.py:353
  (38 shorter events, 1.1 us)
Async XLA Ops:
  0.0 17.0 %copy-start.5 = (f32[1,256]{1,0:T(1,128)S(1)}, f32[1,256]{1,0:T(1,128)}, u32[]{:S(2)}) copy-start(f32[1,256]{1,0:T(1,128)} %constant.155.clone.scale_ref.refs_2_) | copy-start | bytes 3076
  0.0 44.5 %copy-start.9 = (s32[1,1,48]{2,1,0:T(1,128)S(1)}, s32[1,1,48]{2,1,0:T(1,128)}, u32[]{:S(2)}) copy-start(s32[1,1,48]{2,1,0:T(1,128)} %param.12) | copy-start | bytes 580
  0.0 44.5 %copy-start.7 = (s32[1,1,48]{2,1,0:T(1,128)S(1)}, s32[1,1,48]{2,1,0:T(1,128)}, u32[]{:S(2)}) copy-start(s32[1,1,48]{2,1,0:T(1,128)} %param.11) | copy-start | bytes 580
  0.7 2.8 %copy-start = (bf16[1,1,48,256,256]{4,3,2,1,0:T(8,128)(2,1)S(1)}, bf16[1,1,48,256,256]{4,3,2,1,0:T(8,128)(2,1)}, u32[]{:S(2)}) copy-start(bf16[1,1,48,256,256]{4,3,2,1,0:T(8,128)(2,1)} %param.10) | copy-start | bytes 18874372
  3.5 0.7 copy-start.6
  4.1 0.7 copy-start.8
  4.8 3.3 %copy-start.2 = (f32[32,2048]{1,0:T(8,128)S(1)}, f32[32,2048]{1,0:T(8,128)}, u32[]{:S(2)}) copy-start(f32[32,2048]{1,0:T(8,128)} %mine_ref.1) | copy-start | bytes 786436
  4.8 12.2 %copy-start.4 = (bf16[256,256]{1,0:T(8,128)(2,1)S(1)}, bf16[256,256]{1,0:T(8,128)(2,1)}, u32[]{:S(2)}) copy-start(bf16[256,256]{1,0:T(8,128)(2,1)} %constant.154.clone.signs_ref) | copy-start | bytes 393220
  6.7 58.0 %copy-start.3 = (bf16[256,256]{1,0:T(8,128)(2,1)S(1)}, bf16[256,256]{1,0:T(8,128)(2,1)}, u32[]{:S(2)}) copy-start(bf16[256,256]{1,0:T(8,128)(2,1)} %constant.156.clone.refs_1_) | copy-start | bytes 393220
  6.7 3.7 %collective-permute-start = (f32[8,256]{1,0:T(8,128)S(1)}, f32[8,256]{1,0:T(8,128)S(1)}, u32[]{:S(2)}, u32[]{:S(2)}) collective-permute-start(f32[8,256]{1,0:T(8,128)S(1)} %slice.14), channel_id=1, source_target_pairs={{0,2},{1,3},{2,0},{3,1},{4,6},{5,7},{6,4},{7,5},{8,10},{9,11},{10,... | collective-permute-start | bytes 24584 | tf_op jit(solution)/shard_map/ppermute | solution.py:221
  8.1 8.9 %collective-permute-start.5 = (f32[32,2048]{1,0:T(8,128)S(1)}, f32[32,2048]{1,0:T(8,128)S(1)}, u32[]{:S(2)}, u32[]{:S(2)}) collective-permute-start(f32[32,2048]{1,0:T(8,128)S(1)} %copy-done.2), channel_id=1, source_target_pairs={{0,1},{1,0},{2,3},{3,2},{4,5},{5,4},{6,7},{7,6},{8,9},{9,8},{10,11... | collective-permute-start | bytes 786440 | tf_op jit(solution)/shard_map/ppermute | solution.py:245
  10.4 1.2 %collective-permute-start.1 = (f32[8,256]{1,0:T(8,128)S(1)}, f32[8,256]{1,0:T(8,128)S(1)}, u32[]{:S(2)}, u32[]{:S(2)}) collective-permute-start(f32[8,256]{1,0:T(8,128)S(1)} %multiply_select_fusion.2), channel_id=1, source_target_pairs={{0,1},{1,0},{2,3},{3,2},{4,5},{5,4},{6,7},{7,6},{8,9},{9,8},{10,11... | collective-permute-start | bytes 24584 | tf_op jit(solution)/shard_map/ppermute | solution.py:221
  14.6 6.6 %collective-permute-start.2 = (f32[16,256]{1,0:T(8,128)S(1)}, f32[16,256]{1,0:T(8,128)S(1)}, u32[]{:S(2)}, u32[]{:S(2)}) collective-permute-start(f32[16,256]{1,0:T(8,128)S(1)} %scatter_fusion), channel_id=1, source_target_pairs={{0,16},{4,20},{8,24},{12,28},{16,0},{20,4},{24,8},{28,12},{1,17},{... | collective-permute-start | bytes 49160 | tf_op jit(solution)/shard_map/ppermute | solution.py:221
  17.6 12.1 %collective-permute-start.8 = (bf16[528,256]{1,0:T(8,128)(2,1)S(1)}, bf16[528,256]{1,0:T(8,128)(2,1)S(1)}, u32[]{:S(2)}, u32[]{:S(2)}) collective-permute-start(bf16[528,256]{1,0:T(8,128)(2,1)S(1)} %front.1), channel_id=1, source_target_pairs={{0,8},{1,24},{2,0},{3,16},{4,12},{5,28},{6,4},{7,20},{8,9},{9,25},... | collective-permute-start | bytes 811016 | tf_op jit(solution)/shard_map/ppermute | solution.py:245
  17.6 12.1 %collective-permute-start.6 = (bf16[528,256]{1,0:T(8,128)(2,1)S(1)}, bf16[528,256]{1,0:T(8,128)(2,1)S(1)}, u32[]{:S(2)}, u32[]{:S(2)}) collective-permute-start(bf16[528,256]{1,0:T(8,128)(2,1)S(1)} %front.1), channel_id=1, source_target_pairs={{0,0},{1,16},{2,8},{3,24},{4,4},{5,20},{6,12},{7,28},{8,1},{9,17},... | collective-permute-start | bytes 811016 | tf_op jit(solution)/shard_map/ppermute | solution.py:245
  21.3 6.0 %collective-permute-start.3 = (f32[16,256]{1,0:T(8,128)S(1)}, f32[16,256]{1,0:T(8,128)S(1)}, u32[]{:S(2)}, u32[]{:S(2)}) collective-permute-start(f32[16,256]{1,0:T(8,128)S(1)} %multiply_select_fusion.1), channel_id=1, source_target_pairs={{0,8},{4,12},{8,0},{12,4},{16,24},{20,28},{24,16},{28,20},{1,9},{5... | collective-permute-start | bytes 49160 | tf_op jit(solution)/shard_map/ppermute | solution.py:221
  27.3 4.4 %collective-permute-start.4 = (f32[16,256]{1,0:T(8,128)S(1)}, f32[16,256]{1,0:T(8,128)S(1)}, u32[]{:S(2)}, u32[]{:S(2)}) collective-permute-start(f32[16,256]{1,0:T(8,128)S(1)} %multiply_select_fusion), channel_id=1, source_target_pairs={{0,4},{4,0},{8,12},{12,8},{16,20},{20,16},{24,28},{28,24},{1,5},{5... | collective-permute-start | bytes 49160 | tf_op jit(solution)/shard_map/ppermute | solution.py:221
  29.6 9.0 %collective-permute-start.9 = (bf16[528,256]{1,0:T(8,128)(2,1)S(1)}, bf16[528,256]{1,0:T(8,128)(2,1)S(1)}, u32[]{:S(2)}, u32[]{:S(2)}) collective-permute-start(bf16[528,256]{1,0:T(8,128)(2,1)S(1)} %collective-permute-done.8.refs_2_), channel_id=1, source_target_pairs={{0,4},{1,5},{2,6},{3,7},{4,0},{5,1},{6,2},{7,3},{8,12},{9,13},{10,... | collective-permute-start | bytes 811016 | tf_op jit(solution)/shard_map/ppermute | solution.py:245
  29.7 14.8 %collective-permute-start.7 = (bf16[528,256]{1,0:T(8,128)(2,1)S(1)}, bf16[528,256]{1,0:T(8,128)(2,1)S(1)}, u32[]{:S(2)}, u32[]{:S(2)}) collective-permute-start(bf16[528,256]{1,0:T(8,128)(2,1)S(1)} %collective-permute-done.6.refs_0_), channel_id=1, source_target_pairs={{0,4},{1,5},{2,6},{3,7},{4,0},{5,1},{6,2},{7,3},{8,12},{9,13},{10,... | collective-permute-start | bytes 811016 | tf_op jit(solution)/shard_map/ppermute | solution.py:245
  44.5 2.8 %copy-start.1 = (bf16[1,1,48,256,256]{4,3,2,1,0:T(8,128)(2,1)S(1)}, bf16[1,1,48,256,256]{4,3,2,1,0:T(8,128)(2,1)}, u32[]{:S(2)}) copy-start(bf16[1,1,48,256,256]{4,3,2,1,0:T(8,128)(2,1)} %param.10) | copy-start | bytes 18874372
  54.6 4.2 %collective-permute-start.10 = (f32[2,8,32,256]{3,2,1,0:T(8,128)S(1)}, f32[2,8,32,256]{3,2,1,0:T(8,128)S(1)}, u32[]{:S(2)}, u32[]{:S(2)}) collective-permute-start(f32[2,8,32,256]{3,2,1,0:T(8,128)S(1)} %get-tuple-element.14), channel_id=1, source_target_pairs={{0,1},{1,0},{2,3},{3,2},{4,5},{5,4},{6,7},{7,6},{8,9},{9,8},{10,11... | collective-permute-start | bytes 1572872 | tf_op jit(solution)/shard_map/ppermute | solution.py:245
  58.8 5.8 %collective-permute-start.11 = (bf16[8,32,256]{2,1,0:T(8,128)(2,1)S(1)}, bf16[8,32,256]{2,1,0:T(8,128)(2,1)S(1)}, u32[]{:S(2)}, u32[]{:S(2)}) collective-permute-start(bf16[8,32,256]{2,1,0:T(8,128)(2,1)S(1)} %get-tuple-element.16), channel_id=1, source_target_pairs={{0,2},{1,3},{2,0},{3,1},{4,6},{5,7},{6,4},{7,5},{8,10},{9,11},{10,... | collective-permute-start | bytes 393224 | tf_op jit(solution)/shard_map/ppermute | solution.py:245

commit v2 on v1

v2 whole, which is shorter than its diff:
```python
import functools
import math

import jax
import jax.numpy as jnp
import numpy as np
from jax import lax
from jax.experimental import pallas as pl
from jax.experimental.pallas import tpu as pltpu
from jax.sharding import PartitionSpec as P

ROOT_HALF = 1.0 / math.sqrt(2.0)
SIDE_ROWS = 16
CHUNKS = 2
UNROLL = 4
MIB = 2**20


def haar_table(extent):
    matrix = np.eye(extent)
    stride = 1
    while stride < extent:
        for position in range(0, extent, 2 * stride):
            first_row = matrix[position].copy()
            second_row = matrix[position + stride].copy()
            matrix[position] = (first_row + second_row) * ROOT_HALF
            matrix[position + stride] = (first_row - second_row) * ROOT_HALF
        stride = stride * 2
    return matrix


def haar_parts(extent):
    matrix = haar_table(extent)
    scale = np.max(np.abs(matrix), axis=1)
    signs = np.round(matrix / scale[:, None])
    return signs.T, scale[None, :]


def three_terms(value):
    high = value.astype(jnp.bfloat16)
    rest = value - high.astype(jnp.float32)
    middle = rest.astype(jnp.bfloat16)
    low = (rest - middle.astype(jnp.float32)).astype(jnp.bfloat16)
    return high, middle, low


def exact_dot(value, signs):
    return sum(jnp.dot(term, signs, preferred_element_type=jnp.float32) for term in three_terms(value))


def block_forward(columns):
    columns = list(columns)
    stride = 1
    while stride < len(columns):
        for p in range(0, len(columns), 2 * stride):
            u, v = columns[p], columns[p + stride]
            columns[p], columns[p + stride] = (u + v) * ROOT_HALF, (u - v) * ROOT_HALF
        stride *= 2
    return columns


def block_inverse(columns):
    columns = list(columns)
    stride = len(columns) // 2
    while stride >= 1:
        for p in range(0, len(columns), 2 * stride):
            u, v = columns[p], columns[p + stride]
            columns[p], columns[p + stride] = (u + v) * ROOT_HALF, (u - v) * ROOT_HALF
        stride //= 2
    return columns


def front_kernel(core_ref, mine_ref, other_ref, signs_ref, scale_ref, *out_refs, blocks, extent):
    height = mine_ref.shape[0]
    pair = 2 * height
    mine, other = mine_ref[...], other_ref[...]
    first_core = core_ref[0] == 0
    both = jnp.concatenate([jnp.where(first_core, mine, other), jnp.where(first_core, other, mine)], axis=0)
    parts = [both[:, b * extent : (b + 1) * extent] for b in range(blocks)]
    coef = exact_dot(jnp.concatenate(parts, axis=0), signs_ref[...]) * scale_ref[...]
    columns = block_forward([coef[b * pair : (b + 1) * pair, 0:1] for b in range(blocks)])
    lane = lax.broadcasted_iota(jnp.int32, (pair, extent), 1)
    held = blocks // len(out_refs)
    for b in range(blocks):
        column = jnp.zeros_like(columns[0]) if b == 0 else columns[b]
        block = jnp.where(lane == 0, column, coef[b * pair : (b + 1) * pair, :])
        at = b % held * pair
        out_refs[b // held][at : at + pair, :] = block.astype(jnp.bfloat16)
    total = functools.reduce(jnp.add, parts)
    ones = jnp.ones((SIDE_ROWS, extent), jnp.bfloat16)
    first = sum(
        lax.dot_general(ones, term, (((1,), (1,)), ((), ())), preferred_element_type=jnp.float32)
        for term in three_terms(total)
    ) * (1.0 / math.sqrt(blocks * extent))
    high, middle, low = (term.astype(jnp.float32) for term in three_terms(first))
    row = lax.broadcasted_iota(jnp.int32, first.shape, 0)
    side = jnp.where(row == 0, high, jnp.where(row == 1, middle, jnp.where(row == 2, low, 0.0)))
    out_refs[-1][held * pair :, :] = jnp.zeros((SIDE_ROWS, extent), jnp.bfloat16)
    out_refs[-1][held * pair :, 0:pair] = side.astype(jnp.bfloat16)


def edge_kernel(
    place_ref, rows_ref, cols_ref, count_ref, tiles_ref, _, lead_ref, rest_ref, row_ref, order_ref, sizes_ref, *, blocks, owners
):
    extent = tiles_ref.shape[-1]
    lead_ref[...] = jnp.zeros_like(lead_ref)
    rest_ref[...] = jnp.zeros_like(rest_ref)
    row_ref[...] = jnp.zeros_like(row_ref)
    pick = (lax.broadcasted_iota(jnp.int32, (SIDE_ROWS, extent), 1) == 0).astype(jnp.bfloat16)
    x = place_ref[2]

    def visit(slot, sizes):
        row, col = rows_ref[slot], cols_ref[slot]
        owner, block = col // blocks, lax.rem(col, blocks)

        @pl.when((block == 0) & (owner == 0))
        def _():
            lead_ref[pl.ds(row, 1), :] += tiles_ref[slot, 0:SIDE_ROWS, :].astype(jnp.float32)[0:1, :]

        @pl.when((block == 0) & (owner > 0))
        def _():
            at = pl.ds((owner - 1) * blocks + row, 1)
            rest_ref[at, :] += tiles_ref[slot, 0:SIDE_ROWS, :].astype(jnp.float32)[0:1, :]

        @pl.when(row == 0)
        def _():
            column = lax.dot_general(
                pick, tiles_ref[slot], (((1,), (1,)), ((), ())), preferred_element_type=jnp.float32
            )
            row_ref[pl.ds(col, 1), :] += column[0:1, :]

        behind = lax.rem(x - owner + owners, owners)
        side = jnp.where(behind == 0, block, (behind - 1) * blocks + block)
        entry = (slot * 256 + side) * 256 + row
        own = (behind == 0).astype(jnp.int32)
        order_ref[1 - own, jnp.where(own == 1, sizes[0], sizes[1])] = entry
        return sizes[0] + own, sizes[1] + 1 - own

    sizes = lax.fori_loop(0, count_ref[0], visit, (jnp.int32(0), jnp.int32(0)))
    for which in range(2):
        sizes_ref[which] = sizes[which]
        for k in range(UNROLL - 1):
            order_ref[which, sizes[which] + k] = blocks


def corner_kernel(place_ref, lead_ref, partner_ref, rest_ref, row_ref, cols_ref, fixed_ref, *, blocks, owners):
    lead, partner = lead_ref[...], partner_ref[...]
    combined = jnp.where(place_ref[0] == 1, partner - lead, partner + lead) * ROOT_HALF
    lines = [combined] + [rest_ref[i * blocks : (i + 1) * blocks, :] for i in range(owners - 1)]
    lines = block_inverse(lines)
    fixed = row_ref[...]
    index = lax.broadcasted_iota(jnp.int32, fixed.shape, 0)
    lane = lax.broadcasted_iota(jnp.int32, fixed.shape, 1)
    for i, line in enumerate(lines):
        cols_ref[i * blocks : (i + 1) * blocks, :] = line
        fixed = jnp.where((index == i * blocks) & (lane == 0), line[0:1, 0:1], fixed)
    fixed_ref[...] = fixed


def fill_sides(sides, messages, place_ref, chunks, blocks, spans):
    pair = sides.shape[1] // spans
    held = blocks // chunks
    for index, message in enumerate(messages):
        behind, m, chunk = index // (spans * chunks), index // chunks % spans, index % chunks
        rows = pl.ds(pl.multiple_of(place_ref[3 + m] * pair, pair), pair)
        for b in range(held):
            sides[behind * blocks + chunk * held + b, rows, :] = message[b * pair : (b + 1) * pair, :]


def add_products(order_ref, sizes_ref, which, tiles_ref, sides, acc):
    def group(index, _):
        for k in range(UNROLL):
            entry = order_ref[which, index * UNROLL + k]
            slot, side, row = entry >> 16, (entry >> 8) & 255, entry & 255
            acc[row] += jnp.dot(sides[side], tiles_ref[slot], preferred_element_type=jnp.float32)
        return 0

    lax.fori_loop(0, (sizes_ref[which] + UNROLL - 1) // UNROLL, group, 0)


def near_kernel(place_ref, order_ref, sizes_ref, tiles_ref, *refs, blocks, spans, chunks):
    *messages, acc_ref, sides = refs
    fill_sides(sides, messages, place_ref, chunks, blocks, spans)
    acc_ref[...] = jnp.zeros_like(acc_ref)
    add_products(order_ref, sizes_ref, 0, tiles_ref, sides, acc_ref)


def far_kernel(
    place_ref, order_ref, sizes_ref, tiles_ref, near_ref, cols_ref, row_ref, *refs, blocks, owners, spans, chunks
):
    direct, swapped = refs[: spans * chunks], refs[spans * chunks : owners * spans * chunks]
    keep_ref, send_ref, sides, acc, firsts = refs[owners * spans * chunks :]
    extent = tiles_ref.shape[-1]
    pair = sides.shape[1] // spans
    height = pair // 2
    held = blocks // chunks
    x = place_ref[2]
    fill_sides(sides, swapped, place_ref, chunks, blocks, spans)
    messages = (*direct, *swapped)
    for behind in range(owners):
        owner = lax.rem(x - behind + owners, owners)
        for m in range(spans):
            message = messages[(behind * spans + m) * chunks + chunks - 1]
            side = jnp.transpose(message[held * pair :, :].astype(jnp.float32))
            column = side[0:pair, 0:1] + side[0:pair, 1:2] + side[0:pair, 2:3]
            rows = pl.ds(pl.multiple_of(place_ref[3 + m] * pair, pair), pair)
            firsts[owner, rows, :] = jnp.broadcast_to(column, (pair, firsts.shape[2]))
    for i in range(blocks):
        total = near_ref[i]
        for owner in range(owners):
            total += firsts[owner][:, 0:1] * cols_ref[owner * blocks + i : owner * blocks + i + 1, :]
        acc[i] = total
    add_products(order_ref, sizes_ref, 1, tiles_ref, sides, acc)

    lane = lax.broadcasted_iota(jnp.int32, (pair, extent), 1)
    for m in range(spans):
        rows = pl.ds(pl.multiple_of(place_ref[3 + m] * pair, pair), pair)
        total = jnp.zeros((pair, extent), jnp.float32)
        top = jnp.zeros((pair, 1), jnp.float32)
        for behind in range(owners):
            owner = lax.rem(x - behind + owners, owners)
            for b in range(blocks):
                message = messages[(behind * spans + m) * chunks + b // held]
                at = b % held * pair
                line = row_ref[pl.ds(owner * blocks + b, 1), :]
                total += message[at : at + pair, :].astype(jnp.float32) * line
                if b == 0:
                    top += firsts[owner, rows, :][:, 0:1] * line[:, 0:1]
        top += jnp.sum(total, axis=1, keepdims=True)
        acc[0, rows, :] = jnp.where(lane == 0, top, acc[0, rows, :])
    first_core = place_ref[0] == 0
    for i in range(blocks):
        value = acc[i]
        for y in range(spans):
            one = value[y * pair : y * pair + height, :]
            two = value[y * pair + height : (y + 1) * pair, :]
            keep_ref[y, i] = jnp.where(first_core, one, two)
            send_ref[y, i] = jnp.where(first_core, two, one)


def combine_kernel(place_ref, keep_ref, arrived_ref, own_ref, *out_refs):
    spans = keep_ref.shape[0]
    span = place_ref[1]
    own_ref[...] = keep_ref[span] + arrived_ref[span]
    for j, out_ref in enumerate(out_refs, 1):
        at = lax.rem(span + j, spans)
        out_ref[...] = (keep_ref[at] + arrived_ref[at]).astype(jnp.bfloat16)


def back_kernel(own_ref, *refs):
    *arrived, signs_ref, scale_ref, out_ref = refs
    blocks, height, extent = own_ref.shape
    total = own_ref[...]
    for part in arrived:
        total = total + part[...].astype(jnp.float32)
    columns = block_inverse([total[b][:, 0:1] for b in range(blocks)])
    lane = lax.broadcasted_iota(jnp.int32, (height, extent), 1)
    fixed = jnp.concatenate([jnp.where(lane == 0, columns[b], total[b]) for b in range(blocks)], axis=0)
    result = exact_dot(fixed * scale_ref[...], signs_ref[...])
    for b in range(blocks):
        out_ref[:, b * extent : (b + 1) * extent] = result[b * height : (b + 1) * height, :]


def butterfly(value, partner, index, bit):
    active = index % 2**bit == 0
    upper = index // 2**bit % 2 == 1
    combined = jnp.where(upper, partner - value, partner + value) * ROOT_HALF
    return jnp.where(active, combined, value)


def local(sources, tiles, tile_row, tile_col, tile_count):
    n_row, n_col = lax.axis_size("row"), lax.axis_size("col")
    owners = n_row // n_col
    spans = n_col // 2
    extent = tiles.shape[-1]
    slots = tiles.shape[2]
    height = sources.shape[0]
    blocks = sources.shape[1] // extent
    pair = 2 * height
    held = blocks // CHUNKS
    row_index, col_index = lax.axis_index("row"), lax.axis_index("col")
    z, x = row_index // owners, row_index % owners
    span, core = col_index // 2, col_index % 2
    signs, scale = haar_parts(extent)

    def moved(value, to):
        pairs = []
        for a in range(n_row):
            for b in range(n_col):
                zz, xx, yy, cc = to(a // owners, a % owners, b // 2, b % 2)
                pairs.append((a * n_col + b, (zz * owners + xx) * n_col + yy * 2 + cc))
        return lax.ppermute(value, ("row", "col"), pairs)

    def other_core(value):
        return moved(value, lambda zz, xx, yy, cc: (zz, xx, yy, 1 - cc))

    def along_x(value, j):
        return moved(value, lambda zz, xx, yy, cc: (zz, (xx + j) % owners, yy, cc))

    smem = pl.BlockSpec(memory_space=pltpu.SMEM)
    vmem = pl.BlockSpec(memory_space=pltpu.VMEM)

    def call(kernel, name, out_shape, in_specs, out_specs, limit=16, scratch=(), flops=0, moved_bytes=MIB, **sizes):
        return pl.pallas_call(
            functools.partial(kernel, **sizes) if sizes else kernel,
            out_shape=out_shape,
            in_specs=in_specs,
            out_specs=out_specs,
            scratch_shapes=scratch,
            name=name,
            compiler_params=pltpu.CompilerParams(vmem_limit_bytes=limit * MIB),
            cost_estimate=pl.CostEstimate(flops=flops, bytes_accessed=moved_bytes, transcendentals=0),
        )

    def f32(*dims):
        return jax.ShapeDtypeStruct(dims, jnp.float32)

    def bf16(*dims):
        return jax.ShapeDtypeStruct(dims, jnp.bfloat16)

    place = jnp.stack([core, span, x] + [(z - m) % spans for m in range(spans)]).astype(jnp.int32)

    messages = call(
        front_kernel,
        "front",
        [bf16(held * pair + (SIDE_ROWS if q == CHUNKS - 1 else 0), extent) for q in range(CHUNKS)],
        [smem, vmem, vmem, vmem, vmem],
        [vmem] * CHUNKS,
        blocks=blocks,
        extent=extent,
    )(place, sources, other_core(sources), jnp.asarray(signs, jnp.bfloat16), jnp.asarray(scale, jnp.float32))

    direct = [
        moved(messages[q], lambda zz, xx, yy, cc, m=m: (cc * spans + (yy + m) % spans, xx, zz // 2, zz % 2))
        for m in range(spans)
        for q in range(CHUNKS)
    ]
    swapped = [along_x(piece, j) for j in range(1, owners) for piece in direct]

    stack = tiles.reshape(slots, extent, extent)
    rows_flat, cols_flat = tile_row.reshape(-1), tile_col.reshape(-1)
    lead, rest, first_row, order, sizes = call(
        edge_kernel,
        "edges",
        [
            f32(blocks, extent),
            f32((owners - 1) * blocks, extent),
            f32(owners * blocks, extent),
            jax.ShapeDtypeStruct((2, slots + UNROLL), jnp.int32),
            jax.ShapeDtypeStruct((2,), jnp.int32),
        ],
        [smem] * 4 + [vmem, pl.BlockSpec(memory_space=pl.ANY)],
        [vmem] * 3 + [smem] * 2,
        blocks=blocks,
        owners=owners,
    )(place, rows_flat, cols_flat, tile_count.reshape(1), stack, messages[0])

    for bit in reversed(range(1, n_col.bit_length() - 1)):
        step = 2 ** (bit - 1)
        partner = moved(lead, lambda zz, xx, yy, cc, step=step: (zz, xx, yy ^ step, cc))
        lead = butterfly(lead, partner, col_index, bit)
    first_cols, first_row = call(
        corner_kernel,
        "corner",
        [f32(owners * blocks, extent)] * 2,
        [smem] + [vmem] * 4,
        [vmem] * 2,
        blocks=blocks,
        owners=owners,
    )(place, lead, other_core(lead), rest, first_row)
    behind = [first_row] + [along_x(first_row, j) for j in range(1, owners)]
    by_x = []
    for i in range(owners):
        line = behind[0]
        for j in range(1, owners):
            line = jnp.where((x - i) % owners == j, behind[j], line)
        by_x.append(line)
    for bit in reversed(range((n_row // owners).bit_length() - 1)):
        partner = moved(by_x[0], lambda zz, xx, yy, cc, bit=bit: (zz ^ 2**bit, xx, yy, cc))
        by_x[0] = butterfly(by_x[0], partner, z, bit)
    by_x = block_inverse(by_x)
    first_row = by_x[0]
    for i in range(1, owners):
        first_row = jnp.where(x == i, by_x[i], first_row)

    every = (spans * pair, extent)
    work = 2 * slots * spans * pair * extent * extent
    near = call(
        near_kernel,
        "near",
        f32(blocks + 1, *every),
        [smem] * 3 + [vmem] * (1 + len(direct)),
        vmem,
        limit=24,
        scratch=[pltpu.VMEM((blocks, *every), jnp.bfloat16)],
        flops=work // owners,
        moved_bytes=stack.size * 2,
        blocks=blocks,
        spans=spans,
        chunks=CHUNKS,
    )(place, order, sizes, stack, *direct)

    shape = (spans, blocks, height, extent)
    keep, send = call(
        far_kernel,
        "far",
        [f32(*shape)] * 2,
        [smem] * 3 + [vmem] * (4 + len(direct) + len(swapped)),
        [vmem] * 2,
        limit=32,
        scratch=[
            pltpu.VMEM(((owners - 1) * blocks, *every), jnp.bfloat16),
            pltpu.VMEM((blocks + 1, *every), jnp.float32),
            pltpu.VMEM((owners, spans * pair, 128), jnp.float32),
        ],
        flops=work,
        moved_bytes=stack.size * 2,
        blocks=blocks,
        owners=owners,
        spans=spans,
        chunks=CHUNKS,
    )(place, order, sizes, stack, near, first_cols, first_row, *direct, *swapped)

    own, *outgoing = call(
        combine_kernel,
        "combine",
        [f32(*shape[1:])] + [bf16(*shape[1:])] * (spans - 1),
        [smem, vmem, vmem],
        [vmem] * spans,
    )(place, keep, other_core(send))
    arrived = [
        moved(value, lambda zz, xx, yy, cc, j=j: (zz, xx, (yy + j) % spans, cc)) for j, value in enumerate(outgoing, 1)
    ]
    return call(back_kernel, "back", f32(*sources.shape), [vmem] * (spans + 2), vmem)(
        own, *arrived, jnp.asarray(signs.T, jnp.bfloat16), jnp.asarray(scale, jnp.float32)
    )


def solution(mesh):
    return jax.shard_map(
        local,
        mesh=mesh,
        in_specs=(
            P("col", "row"),
            P("row", "col", None, None, None),
            P("row", "col", None),
            P("row", "col", None),
            P("row", "col"),
        ),
        out_specs=P("col", "row"),
        check_vma=False,
    )
```

time: 66.4 us -> 61 us (0.919)
  the two profiles are of different devices: /device:TPU:8 before, /device:TPU:0 now
where the time goes in v2:
time: 61 us; the launch traced here: 60.7 us
  starting transfers between devices  25.5 us (42%)
  waiting for transfers between devices  14.8 us (24%)
  Pallas kernels  10 us (16%)
  local copies, waits for them, and re-layouts  9.51 us (16%)
  between operations  0.84 us (1%)
    ppermute x16, starting transfers between devices, moved(): return lax.ppermute(value, ('row', 'col'), pairs)  25.5 us
    ppermute x16, waiting for transfers between devices, moved(): return lax.ppermute(value, ('row', 'col'), pairs)  14.8 us
    unnamed x22, local copies, waits for them, and re-layouts  9.42 us
    pallas_call x1, Pallas kernels, local(): call(far_kernel, 'far', [f32(*shape)] * 2, [smem] * 3 + [vmem] * (4 + len...  2.6 us
    pallas_call x1, Pallas kernels, local(): call(edge_kernel, 'edges', [f32(blocks, extent), f32((owners - 1) * block...  2.43 us
    pallas_call x1, Pallas kernels, local(): call(near_kernel, 'near', f32(blocks + 1, *every), [smem] * 3 + [vmem] *...  1.7 us
  transfers between devices with their start and end apart: 16, of which 8 were waited for; matrix products, arithmetic and copies ran while one was open for 0% of the time, Pallas kernels for 3%

profile of v2, /device:TPU:0, one launch (start us, length us, event | category | flops | bytes accessed | tf_op | source)
XLA Modules:
  0.0 60.7 jit_solution(14017379083283201045)
XLA Ops:
  1.8 0.9 %copy-done.2 = f32[32,2048]{1,0:T(8,128)S(1)} copy-done((f32[32,2048]{1,0:T(8,128)S(1)}, f32[32,2048]{1,0:T(8,128)}, u32[]{:S(2)}) %copy-start.2) | copy-done | bytes 262168
  2.8 0.9 %copy-done.4 = bf16[256,256]{1,0:T(8,128)(2,1)S(1)} copy-done((bf16[256,256]{1,0:T(8,128)(2,1)S(1)}, bf16[256,256]{1,0:T(8,128)(2,1)}, u32[]{:S(2)}) %copy-start.4) | copy-done | bytes 131096
  4.4 1.0 %front.1 = (bf16[256,256]{1,0:T(8,128)(2,1)S(1)}, bf16[272,256]{1,0:T(8,128)(2,1)S(1)}) custom-call(s32[5]{0:T(128)S(1)} %stack.23.core_ref.place_ref, f32[32,2048]{1,0:T(8,128)S(1)} %copy-done.2, f32[32,2048]{1,0:T(8,128)S(1)} %collective-permute-done.other_ref, bf16[256,256]{1,0:T(8,128)(2,1)S(1)} %copy-done.4, f32[1,256]{1,0:T(1,128)S(1)} %copy-done.5), custom_call_target="tpu_custom_call" | custom-call | bytes 1048576 | tf_op jit(solution)/shard_map/front/pallas_call | solution.py:323
  5.4 2.8 %copy-done = bf16[1,1,48,256,256]{4,3,2,1,0:T(8,128)(2,1)S(1)} copy-done((bf16[1,1,48,256,256]{4,3,2,1,0:T(8,128)(2,1)S(1)}, bf16[1,1,48,256,256]{4,3,2,1,0:T(8,128)(2,1)}, u32[]{:S(2)}) %copy-start) | copy-done | bytes 6291480
  9.5 2.4 %edges.1 = (f32[8,256]{1,0:T(8,128)S(1)}, f32[8,256]{1,0:T(8,128)S(1)}, f32[16,256]{1,0:T(8,128)S(1)}, s32[2,52]{1,0:T(2,128)S(1)}, s32[2]{0:T(128)S(1)}) custom-call(s32[5]{0:T(128)S(1)} %stack.23.core_ref.place_ref, s32[48]{0:T(128)S(1)} %bitcast.15, s32[48]{0:T(128)S(1)} %bitcast.16, s32[1]{0:T(128)} %bitcast.9.count_ref, ...), custom_call_target="tpu_custom_call" | custom-call | bytes 1048576 | tf_op jit(solution)/shard_map/edges/pallas_call | solution.py:342
  11.9 2.3 %collective-permute-start.5 = (f32[8,256]{1,0:T(8,128)S(1)}, f32[8,256]{1,0:T(8,128)S(1)}, u32[]{:S(2)}, u32[]{:S(2)}) collective-permute-start(f32[8,256]{1,0:T(8,128)S(1)} %get-tuple-element.22), channel_id=1, source_target_pairs={{0,2},{1,3},{2,0},{3,1},{4,6},{5,7},{6,4},{7,5},{8,10},{9,11},{10,... | collective-permute-start | bytes 24584 | tf_op jit(solution)/shard_map/ppermute | solution.py:292
  14.3 1.6 %collective-permute-done.5 = f32[8,256]{1,0:T(8,128)S(1)} collective-permute-done((f32[8,256]{1,0:T(8,128)S(1)}, f32[8,256]{1,0:T(8,128)S(1)}, u32[]{:S(2)}, u32[]{:S(2)}) %collective-permute-start.5) | collective-permute-done | bytes 8224 | tf_op jit(solution)/shard_map/ppermute | solution.py:292
  15.9 1.2 %collective-permute-done.6.partner_ref = f32[8,256]{1,0:T(8,128)S(1)} collective-permute-done((f32[8,256]{1,0:T(8,128)S(1)}, f32[8,256]{1,0:T(8,128)S(1)}, u32[]{:S(2)}, u32[]{:S(2)}) %collective-permute-start.6) | collective-permute-done | bytes 8224 | tf_op jit(solution)/shard_map/ppermute | solution.py:292
  17.7 2.7 %collective-permute-start.7 = (f32[16,256]{1,0:T(8,128)S(1)}, f32[16,256]{1,0:T(8,128)S(1)}, u32[]{:S(2)}, u32[]{:S(2)}) collective-permute-start(f32[16,256]{1,0:T(8,128)S(1)} %get-tuple-element.26), channel_id=1, source_target_pairs={{0,4},{1,5},{2,6},{3,7},{4,0},{5,1},{6,2},{7,3},{8,12},{9,13},{10,... | collective-permute-start | bytes 49160 | tf_op jit(solution)/shard_map/ppermute | solution.py:292
  20.4 1.7 %collective-permute-done.7 = f32[16,256]{1,0:T(8,128)S(1)} collective-permute-done((f32[16,256]{1,0:T(8,128)S(1)}, f32[16,256]{1,0:T(8,128)S(1)}, u32[]{:S(2)}, u32[]{:S(2)}) %collective-permute-start.7) | collective-permute-done | bytes 16416 | tf_op jit(solution)/shard_map/ppermute | solution.py:292
  22.1 2.4 %collective-permute-start.8 = (f32[16,256]{1,0:T(8,128)S(1)}, f32[16,256]{1,0:T(8,128)S(1)}, u32[]{:S(2)}, u32[]{:S(2)}) collective-permute-start(f32[16,256]{1,0:T(8,128)S(1)} %broadcast_select_fusion), channel_id=1, source_target_pairs={{0,16},{1,17},{2,18},{3,19},{4,20},{5,21},{6,22},{7,23},{8,24},{9,... | collective-permute-start | bytes 49160 | tf_op jit(solution)/shard_map/ppermute | solution.py:292
  24.5 2.3 %collective-permute-start.3 = (bf16[256,256]{1,0:T(8,128)(2,1)S(1)}, bf16[256,256]{1,0:T(8,128)(2,1)S(1)}, u32[]{:S(2)}, u32[]{:S(2)}) collective-permute-start(bf16[256,256]{1,0:T(8,128)(2,1)S(1)} %get-tuple-element.18._), channel_id=1, source_target_pairs={{0,8},{1,24},{2,0},{3,16},{4,12},{5,28},{6,4},{7,20},{8,9},{9,25},... | collective-permute-start | bytes 393224 | tf_op jit(solution)/shard_map/ppermute | solution.py:292
  27.5 2.6 %collective-permute-start.4 = (bf16[272,256]{1,0:T(8,128)(2,1)S(1)}, bf16[272,256]{1,0:T(8,128)(2,1)S(1)}, u32[]{:S(2)}, u32[]{:S(2)}) collective-permute-start(bf16[272,256]{1,0:T(8,128)(2,1)S(1)} %get-tuple-element.21), channel_id=1, source_target_pairs={{0,8},{1,24},{2,0},{3,16},{4,12},{5,28},{6,4},{7,20},{8,9},{9,25},... | collective-permute-start | bytes 417800 | tf_op jit(solution)/shard_map/ppermute | solution.py:292
  30.8 4.7 %collective-permute-start.9 = (f32[16,256]{1,0:T(8,128)S(1)}, f32[16,256]{1,0:T(8,128)S(1)}, u32[]{:S(2)}, u32[]{:S(2)}) collective-permute-start(f32[16,256]{1,0:T(8,128)S(1)} %multiply_select_fusion.1), channel_id=1, source_target_pairs={{0,8},{1,9},{2,10},{3,11},{4,12},{5,13},{6,14},{7,15},{8,0},{9,1},... | collective-permute-start | bytes 49160 | tf_op jit(solution)/shard_map/ppermute | solution.py:292
  35.5 2.0 %collective-permute-start.12 = (bf16[256,256]{1,0:T(8,128)(2,1)S(1)}, bf16[256,256]{1,0:T(8,128)(2,1)S(1)}, u32[]{:S(2)}, u32[]{:S(2)}) collective-permute-start(bf16[256,256]{1,0:T(8,128)(2,1)S(1)} %collective-permute-done.3.refs_2_), channel_id=1, source_target_pairs={{0,4},{1,5},{2,6},{3,7},{4,0},{5,1},{6,2},{7,3},{8,12},{9,13},{10,... | collective-permute-start | bytes 393224 | tf_op jit(solution)/shard_map/ppermute | solution.py:292
  37.6 2.0 %collective-permute-start.13 = (bf16[272,256]{1,0:T(8,128)(2,1)S(1)}, bf16[272,256]{1,0:T(8,128)(2,1)S(1)}, u32[]{:S(2)}, u32[]{:S(2)}) collective-permute-start(bf16[272,256]{1,0:T(8,128)(2,1)S(1)} %collective-permute-done.4.refs_3_), channel_id=1, source_target_pairs={{0,4},{1,5},{2,6},{3,7},{4,0},{5,1},{6,2},{7,3},{8,12},{9,13},{10,... | collective-permute-start | bytes 417800 | tf_op jit(solution)/shard_map/ppermute | solution.py:292
  39.6 3.2 %collective-permute-done.9 = f32[16,256]{1,0:T(8,128)S(1)} collective-permute-done((f32[16,256]{1,0:T(8,128)S(1)}, f32[16,256]{1,0:T(8,128)S(1)}, u32[]{:S(2)}, u32[]{:S(2)}) %collective-permute-start.9) | collective-permute-done | bytes 16416 | tf_op jit(solution)/shard_map/ppermute | solution.py:292
  42.9 2.8 %copy-done.1 = bf16[1,1,48,256,256]{4,3,2,1,0:T(8,128)(2,1)S(1)} copy-done((bf16[1,1,48,256,256]{4,3,2,1,0:T(8,128)(2,1)S(1)}, bf16[1,1,48,256,256]{4,3,2,1,0:T(8,128)(2,1)}, u32[]{:S(2)}) %copy-start.1) | copy-done | bytes 6291480
  45.6 1.7 %near.1.near_ref = f32[9,128,256]{2,1,0:T(8,128)S(1)} custom-call(s32[5]{0:T(128)S(1)} %stack.23.core_ref.place_ref, s32[2,52]{1,0:T(2,128)S(1)} %get-tuple-element.19.order_ref, s32[2]{0:T(128)S(1)} %get-tuple-element.20.sizes_ref, bf16[48,256,256]{2,1,0:T(8,128)(2,1)S(1)} %bitcast.11, bf16[256,256]{1,0:T(8,128)(2,1)S(1)} %collective-permute-done.1.refs_0_, ...), custom_call_target="tpu_custom_call" | custom-call | flops 402653184 | bytes 6291456 | tf_op jit(solution)/shard_map/near/pallas_call | solution.py:388
  48.2 2.6 %far.1 = (f32[2,8,32,256]{3,2,1,0:T(8,128)S(1)}, f32[2,8,32,256]{3,2,1,0:T(8,128)S(1)}) custom-call(s32[5]{0:T(128)S(1)} %stack.23.core_ref.place_ref, s32[2,52]{1,0:T(2,128)S(1)} %get-tuple-element.19.order_ref, s32[2]{0:T(128)S(1)} %get-tuple-element.20.sizes_ref, bf16[48,256,256]{2,1,0:T(8,128)(2,1)S(1)} %bitcast.14, f32[9,128,256]{2,1,0:T(8,128)S(1)} %near.1.near_ref, ...), custom_call_target="tpu_custom_call" | custom-call | flops 805306368 | bytes 6291456 | tf_op jit(solution)/shard_map/far/pallas_call | solution.py:404
  50.9 1.9 %collective-permute-done.14.arrived_ref = f32[2,8,32,256]{3,2,1,0:T(8,128)S(1)} collective-permute-done((f32[2,8,32,256]{3,2,1,0:T(8,128)S(1)}, f32[2,8,32,256]{3,2,1,0:T(8,128)S(1)}, u32[]{:S(2)}, u32[]{:S(2)}) %collective-permute-start.14) | collective-permute-done | bytes 524320 | tf_op jit(solution)/shard_map/ppermute | solution.py:292
  53.4 2.4 %collective-permute-start.15 = (bf16[8,32,256]{2,1,0:T(8,128)(2,1)S(1)}, bf16[8,32,256]{2,1,0:T(8,128)(2,1)S(1)}, u32[]{:S(2)}, u32[]{:S(2)}) collective-permute-start(bf16[8,32,256]{2,1,0:T(8,128)(2,1)S(1)} %get-tuple-element.30), channel_id=1, source_target_pairs={{0,2},{1,3},{2,0},{3,1},{4,6},{5,7},{6,4},{7,5},{8,10},{9,11},{10,... | collective-permute-start | bytes 393224 | tf_op jit(solution)/shard_map/ppermute | solution.py:292
  55.8 3.8 %collective-permute-done.15.refs_0_ = bf16[8,32,256]{2,1,0:T(8,128)(2,1)S(1)} collective-permute-done((bf16[8,32,256]{2,1,0:T(8,128)(2,1)S(1)}, bf16[8,32,256]{2,1,0:T(8,128)(2,1)S(1)}, u32[]{:S(2)}, u32[]{:S(2)}) %collective-permute-start.15) | collective-permute-done | bytes 131104 | tf_op jit(solution)/shard_map/ppermute | solution.py:292
  59.6 1.0 %back.1 = f32[32,2048]{1,0:T(8,128)} custom-call(f32[8,32,256]{2,1,0:T(8,128)S(1)} %get-tuple-element.29.own_ref, bf16[8,32,256]{2,1,0:T(8,128)(2,1)S(1)} %collective-permute-done.15.refs_0_, bf16[256,256]{1,0:T(8,128)(2,1)S(1)} %copy-done.3, f32[1,256]{1,0:T(1,128)S(1)} %copy-done.6), custom_call_target="tpu_custom_call" | custom-call | bytes 1048576 | tf_op jit(solution)/shard_map/back/pallas_call | solution.py:434
  (43 shorter events, 6.8 us)
Async XLA Ops:
  0.0 1.8 %collective-permute-start = (f32[32,2048]{1,0:T(8,128)}, f32[32,2048]{1,0:T(8,128)S(1)}, u32[]{:S(2)}, u32[]{:S(2)}) collective-permute-start(f32[32,2048]{1,0:T(8,128)} %mine_ref.1), channel_id=1, source_target_pairs={{0,1},{1,0},{2,3},{3,2},{4,5},{5,4},{6,7},{7,6},{8,9},{9,8},{10,11... | collective-permute-start | bytes 786440 | tf_op jit(solution)/shard_map/ppermute | solution.py:292
  1.8 0.9 %copy-start.2 = (f32[32,2048]{1,0:T(8,128)S(1)}, f32[32,2048]{1,0:T(8,128)}, u32[]{:S(2)}) copy-start(f32[32,2048]{1,0:T(8,128)} %mine_ref.1) | copy-start | bytes 786436
  2.8 0.9 %copy-start.4 = (bf16[256,256]{1,0:T(8,128)(2,1)S(1)}, bf16[256,256]{1,0:T(8,128)(2,1)}, u32[]{:S(2)}) copy-start(bf16[256,256]{1,0:T(8,128)(2,1)} %constant.114.clone.signs_ref) | copy-start | bytes 393220
  5.4 2.8 %copy-start = (bf16[1,1,48,256,256]{4,3,2,1,0:T(8,128)(2,1)S(1)}, bf16[1,1,48,256,256]{4,3,2,1,0:T(8,128)(2,1)}, u32[]{:S(2)}) copy-start(bf16[1,1,48,256,256]{4,3,2,1,0:T(8,128)(2,1)} %param.10) | copy-start | bytes 18874372
  9.5 38.7 %slice-start = ((s8[6291456]{0:T(1024)(128)(4,1)}), s8[2097152]{0:T(1024)(128)(4,1)S(1)}, s32[]{:S(2)}) async-start(s8[6291456]{0:T(1024)(128)(4,1)} %bitcast.12), calls=%async_computation | async-start | bytes 4194304
  11.9 3.9 %collective-permute-start.5 = (f32[8,256]{1,0:T(8,128)S(1)}, f32[8,256]{1,0:T(8,128)S(1)}, u32[]{:S(2)}, u32[]{:S(2)}) collective-permute-start(f32[8,256]{1,0:T(8,128)S(1)} %get-tuple-element.22), channel_id=1, source_target_pairs={{0,2},{1,3},{2,0},{3,1},{4,6},{5,7},{6,4},{7,5},{8,10},{9,11},{10,... | collective-permute-start | bytes 24584 | tf_op jit(solution)/shard_map/ppermute | solution.py:292
  15.9 1.2 %collective-permute-start.6 = (f32[8,256]{1,0:T(8,128)S(1)}, f32[8,256]{1,0:T(8,128)S(1)}, u32[]{:S(2)}, u32[]{:S(2)}) collective-permute-start(f32[8,256]{1,0:T(8,128)S(1)} %multiply_select_fusion.2.lead_ref), channel_id=1, source_target_pairs={{0,1},{1,0},{2,3},{3,2},{4,5},{5,4},{6,7},{7,6},{8,9},{9,8},{10,11... | collective-permute-start | bytes 24584 | tf_op jit(solution)/shard_map/ppermute | solution.py:292
  17.7 4.4 %collective-permute-start.7 = (f32[16,256]{1,0:T(8,128)S(1)}, f32[16,256]{1,0:T(8,128)S(1)}, u32[]{:S(2)}, u32[]{:S(2)}) collective-permute-start(f32[16,256]{1,0:T(8,128)S(1)} %get-tuple-element.26), channel_id=1, source_target_pairs={{0,4},{1,5},{2,6},{3,7},{4,0},{5,1},{6,2},{7,3},{8,12},{9,13},{10,... | collective-permute-start | bytes 49160 | tf_op jit(solution)/shard_map/ppermute | solution.py:292
  22.1 8.7 %collective-permute-start.8 = (f32[16,256]{1,0:T(8,128)S(1)}, f32[16,256]{1,0:T(8,128)S(1)}, u32[]{:S(2)}, u32[]{:S(2)}) collective-permute-start(f32[16,256]{1,0:T(8,128)S(1)} %broadcast_select_fusion), channel_id=1, source_target_pairs={{0,16},{1,17},{2,18},{3,19},{4,20},{5,21},{6,22},{7,23},{8,24},{9,... | collective-permute-start | bytes 49160 | tf_op jit(solution)/shard_map/ppermute | solution.py:292
  24.5 11.0 %collective-permute-start.3 = (bf16[256,256]{1,0:T(8,128)(2,1)S(1)}, bf16[256,256]{1,0:T(8,128)(2,1)S(1)}, u32[]{:S(2)}, u32[]{:S(2)}) collective-permute-start(bf16[256,256]{1,0:T(8,128)(2,1)S(1)} %get-tuple-element.18._), channel_id=1, source_target_pairs={{0,8},{1,24},{2,0},{3,16},{4,12},{5,28},{6,4},{7,20},{8,9},{9,25},... | collective-permute-start | bytes 393224 | tf_op jit(solution)/shard_map/ppermute | solution.py:292
  26.8 10.7 %collective-permute-start.1 = (bf16[256,256]{1,0:T(8,128)(2,1)S(1)}, bf16[256,256]{1,0:T(8,128)(2,1)S(1)}, u32[]{:S(2)}, u32[]{:S(2)}) collective-permute-start(bf16[256,256]{1,0:T(8,128)(2,1)S(1)} %get-tuple-element.18._), channel_id=1, source_target_pairs={{0,0},{1,16},{2,8},{3,24},{4,4},{5,20},{6,12},{7,28},{8,1},{9,17},... | collective-permute-start | bytes 393224 | tf_op jit(solution)/shard_map/ppermute | solution.py:292
  27.5 10.1 %collective-permute-start.4 = (bf16[272,256]{1,0:T(8,128)(2,1)S(1)}, bf16[272,256]{1,0:T(8,128)(2,1)S(1)}, u32[]{:S(2)}, u32[]{:S(2)}) collective-permute-start(bf16[272,256]{1,0:T(8,128)(2,1)S(1)} %get-tuple-element.21), channel_id=1, source_target_pairs={{0,8},{1,24},{2,0},{3,16},{4,12},{5,28},{6,4},{7,20},{8,9},{9,25},... | collective-permute-start | bytes 417800 | tf_op jit(solution)/shard_map/ppermute | solution.py:292
  30.1 9.5 %collective-permute-start.2 = (bf16[272,256]{1,0:T(8,128)(2,1)S(1)}, bf16[272,256]{1,0:T(8,128)(2,1)S(1)}, u32[]{:S(2)}, u32[]{:S(2)}) collective-permute-start(bf16[272,256]{1,0:T(8,128)(2,1)S(1)} %get-tuple-element.21), channel_id=1, source_target_pairs={{0,0},{1,16},{2,8},{3,24},{4,4},{5,20},{6,12},{7,28},{8,1},{9,17},... | collective-permute-start | bytes 417800 | tf_op jit(solution)/shard_map/ppermute | solution.py:292
  30.8 12.0 %collective-permute-start.9 = (f32[16,256]{1,0:T(8,128)S(1)}, f32[16,256]{1,0:T(8,128)S(1)}, u32[]{:S(2)}, u32[]{:S(2)}) collective-permute-start(f32[16,256]{1,0:T(8,128)S(1)} %multiply_select_fusion.1), channel_id=1, source_target_pairs={{0,8},{1,9},{2,10},{3,11},{4,12},{5,13},{6,14},{7,15},{8,0},{9,1},... | collective-permute-start | bytes 49160 | tf_op jit(solution)/shard_map/ppermute | solution.py:292
  35.5 11.9 %collective-permute-start.12 = (bf16[256,256]{1,0:T(8,128)(2,1)S(1)}, bf16[256,256]{1,0:T(8,128)(2,1)S(1)}, u32[]{:S(2)}, u32[]{:S(2)}) collective-permute-start(bf16[256,256]{1,0:T(8,128)(2,1)S(1)} %collective-permute-done.3.refs_2_), channel_id=1, source_target_pairs={{0,4},{1,5},{2,6},{3,7},{4,0},{5,1},{6,2},{7,3},{8,12},{9,13},{10,... | collective-permute-start | bytes 393224 | tf_op jit(solution)/shard_map/ppermute | solution.py:292
  37.5 9.9 %collective-permute-start.10 = (bf16[256,256]{1,0:T(8,128)(2,1)S(1)}, bf16[256,256]{1,0:T(8,128)(2,1)S(1)}, u32[]{:S(2)}, u32[]{:S(2)}) collective-permute-start(bf16[256,256]{1,0:T(8,128)(2,1)S(1)} %collective-permute-done.1.refs_0_), channel_id=1, source_target_pairs={{0,4},{1,5},{2,6},{3,7},{4,0},{5,1},{6,2},{7,3},{8,12},{9,13},{10,... | collective-permute-start | bytes 393224 | tf_op jit(solution)/shard_map/ppermute | solution.py:292
  37.6 9.8 %collective-permute-start.13 = (bf16[272,256]{1,0:T(8,128)(2,1)S(1)}, bf16[272,256]{1,0:T(8,128)(2,1)S(1)}, u32[]{:S(2)}, u32[]{:S(2)}) collective-permute-start(bf16[272,256]{1,0:T(8,128)(2,1)S(1)} %collective-permute-done.4.refs_3_), channel_id=1, source_target_pairs={{0,4},{1,5},{2,6},{3,7},{4,0},{5,1},{6,2},{7,3},{8,12},{9,13},{10,... | collective-permute-start | bytes 417800 | tf_op jit(solution)/shard_map/ppermute | solution.py:292
  39.6 8.6 %collective-permute-start.11 = (bf16[272,256]{1,0:T(8,128)(2,1)S(1)}, bf16[272,256]{1,0:T(8,128)(2,1)S(1)}, u32[]{:S(2)}, u32[]{:S(2)}) collective-permute-start(bf16[272,256]{1,0:T(8,128)(2,1)S(1)} %collective-permute-done.2.refs_1_), channel_id=1, source_target_pairs={{0,4},{1,5},{2,6},{3,7},{4,0},{5,1},{6,2},{7,3},{8,12},{9,13},{10,... | collective-permute-start | bytes 417800 | tf_op jit(solution)/shard_map/ppermute | solution.py:292
  42.8 2.8 %copy-start.1 = (bf16[1,1,48,256,256]{4,3,2,1,0:T(8,128)(2,1)S(1)}, bf16[1,1,48,256,256]{4,3,2,1,0:T(8,128)(2,1)}, u32[]{:S(2)}) copy-start(bf16[1,1,48,256,256]{4,3,2,1,0:T(8,128)(2,1)} %param.10) | copy-start | bytes 18874372
  45.6 2.6 %slice-start.1 = ((s8[6291456]{0:T(1024)(128)(4,1)}), s8[4194304]{0:T(1024)(128)(4,1)S(1)}, s32[]{:S(2)}) async-start(s8[6291456]{0:T(1024)(128)(4,1)} %bitcast.12), calls=%async_computation.1 | async-start | bytes 8388608
  47.3 12.3 %copy-start.3 = (bf16[256,256]{1,0:T(8,128)(2,1)S(1)}, bf16[256,256]{1,0:T(8,128)(2,1)}, u32[]{:S(2)}) copy-start(bf16[256,256]{1,0:T(8,128)(2,1)} %constant.116.clone.refs_1_) | copy-start | bytes 393220
  47.4 12.3 %copy-start.6 = (f32[1,256]{1,0:T(1,128)S(1)}, f32[1,256]{1,0:T(1,128)}, u32[]{:S(2)}) copy-start(f32[1,256]{1,0:T(1,128)} %constant.115.clone.scale_ref.refs_2_) | copy-start | bytes 3076
  50.8 2.0 %collective-permute-start.14 = (f32[2,8,32,256]{3,2,1,0:T(8,128)S(1)}, f32[2,8,32,256]{3,2,1,0:T(8,128)S(1)}, u32[]{:S(2)}, u32[]{:S(2)}) collective-permute-start(f32[2,8,32,256]{3,2,1,0:T(8,128)S(1)} %get-tuple-element.28), channel_id=1, source_target_pairs={{0,1},{1,0},{2,3},{3,2},{4,5},{5,4},{6,7},{7,6},{8,9},{9,8},{10,11... | collective-permute-start | bytes 1572872 | tf_op jit(solution)/shard_map/ppermute | solution.py:292
  53.4 6.2 %collective-permute-start.15 = (bf16[8,32,256]{2,1,0:T(8,128)(2,1)S(1)}, bf16[8,32,256]{2,1,0:T(8,128)(2,1)S(1)}, u32[]{:S(2)}, u32[]{:S(2)}) collective-permute-start(bf16[8,32,256]{2,1,0:T(8,128)(2,1)S(1)} %get-tuple-element.30), channel_id=1, source_target_pairs={{0,2},{1,3},{2,0},{3,1},{4,6},{5,7},{6,4},{7,5},{8,10},{9,11},{10,... | collective-permute-start | bytes 393224 | tf_op jit(solution)/shard_map/ppermute | solution.py:292
  (3 other events, 2.0 us)

commit v3 on v2

--- a/solution.py
+++ b/solution.py
@@ -3,7 +3,6 @@
 
 import jax
 import jax.numpy as jnp
-import numpy as np
 from jax import lax
 from jax.experimental import pallas as pl
 from jax.experimental.pallas import tpu as pltpu
@@ -16,24 +15,18 @@
 MIB = 2**20
 
 
-def haar_table(extent):
-    matrix = np.eye(extent)
-    stride = 1
-    while stride < extent:
-        for position in range(0, extent, 2 * stride):
-            first_row = matrix[position].copy()
-            second_row = matrix[position + stride].copy()
-            matrix[position] = (first_row + second_row) * ROOT_HALF
-            matrix[position + stride] = (first_row - second_row) * ROOT_HALF
-        stride = stride * 2
-    return matrix
-
-
-def haar_parts(extent):
-    matrix = haar_table(extent)
-    scale = np.max(np.abs(matrix), axis=1)
-    signs = np.round(matrix / scale[:, None])
-    return signs.T, scale[None, :]
+def haar_parts(extent, transposed):
+    k = lax.broadcasted_iota(jnp.int32, (extent, extent), 1 if transposed else 0)
+    n = lax.broadcasted_iota(jnp.int32, (extent, extent), 0 if transposed else 1)
+    stride = jnp.where(n == 0, extent, n & -n)
+    signs = jnp.where((k ^ n) < 2 * stride, jnp.where((k & stride) == 0, 1.0, -1.0), 0.0)
+    n = lax.broadcasted_iota(jnp.int32, (1, extent), 1)
+    scale = jnp.full((1, extent), 1.0 / math.sqrt(extent), jnp.float32)
+    level = 1
+    while level < extent:
+        scale = jnp.where((n & -n) == level, 1.0 / math.sqrt(2 * level), scale)
+        level *= 2
+    return signs.astype(jnp.bfloat16), scale
 
 
 def three_terms(value):
@@ -70,14 +63,19 @@
     return columns
 
 
-def front_kernel(core_ref, mine_ref, other_ref, signs_ref, scale_ref, *out_refs, blocks, extent):
+def front_kernel(core_ref, sources_ref, other_ref, *refs, blocks, extent):
+    *out_refs, mine_ref, sem = refs
+    copy = pltpu.make_async_copy(sources_ref, mine_ref, sem)
+    copy.start()
     height = mine_ref.shape[0]
     pair = 2 * height
+    signs, scale = haar_parts(extent, False)
+    copy.wait()
     mine, other = mine_ref[...], other_ref[...]
     first_core = core_ref[0] == 0
     both = jnp.concatenate([jnp.where(first_core, mine, other), jnp.where(first_core, other, mine)], axis=0)
     parts = [both[:, b * extent : (b + 1) * extent] for b in range(blocks)]
-    coef = exact_dot(jnp.concatenate(parts, axis=0), signs_ref[...]) * scale_ref[...]
+    coef = exact_dot(jnp.concatenate(parts, axis=0), signs) * scale
     columns = block_forward([coef[b * pair : (b + 1) * pair, 0:1] for b in range(blocks)])
     lane = lax.broadcasted_iota(jnp.int32, (pair, extent), 1)
     held = blocks // len(out_refs)
@@ -100,50 +98,85 @@
 
 
 def edge_kernel(
-    place_ref, rows_ref, cols_ref, count_ref, tiles_ref, _, lead_ref, rest_ref, row_ref, order_ref, sizes_ref, *, blocks, owners
+    place_ref,
+    rows_ref,
+    cols_ref,
+    count_ref,
+    tiles_ref,
+    lead_ref,
+    rest_ref,
+    row_ref,
+    order_ref,
+    sizes_ref,
+    strips,
+    held,
+    strip_sem,
+    held_sems,
+    *,
+    blocks,
+    owners,
 ):
     extent = tiles_ref.shape[-1]
+    count = count_ref[0]
+    x = place_ref[2]
+    strip_copy = pltpu.make_async_copy(tiles_ref.at[:, 0:SIDE_ROWS, :], strips, strip_sem)
+    strip_copy.start()
     lead_ref[...] = jnp.zeros_like(lead_ref)
     rest_ref[...] = jnp.zeros_like(rest_ref)
     row_ref[...] = jnp.zeros_like(row_ref)
     pick = (lax.broadcasted_iota(jnp.int32, (SIDE_ROWS, extent), 1) == 0).astype(jnp.bfloat16)
-    x = place_ref[2]
+
+    def tile_copy(slot):
+        return pltpu.make_async_copy(tiles_ref.at[slot], held.at[slot], held_sems.at[slot])
 
     def visit(slot, sizes):
         row, col = rows_ref[slot], cols_ref[slot]
         owner, block = col // blocks, lax.rem(col, blocks)
 
-        @pl.when((block == 0) & (owner == 0))
-        def _():
-            lead_ref[pl.ds(row, 1), :] += tiles_ref[slot, 0:SIDE_ROWS, :].astype(jnp.float32)[0:1, :]
-
-        @pl.when((block == 0) & (owner > 0))
-        def _():
-            at = pl.ds((owner - 1) * blocks + row, 1)
-            rest_ref[at, :] += tiles_ref[slot, 0:SIDE_ROWS, :].astype(jnp.float32)[0:1, :]
-
         @pl.when(row == 0)
         def _():
-            column = lax.dot_general(
-                pick, tiles_ref[slot], (((1,), (1,)), ((), ())), preferred_element_type=jnp.float32
-            )
-            row_ref[pl.ds(col, 1), :] += column[0:1, :]
+            tile_copy(slot).start()
 
         behind = lax.rem(x - owner + owners, owners)
+        own = (behind == 0).astype(jnp.int32)
         side = jnp.where(behind == 0, block, (behind - 1) * blocks + block)
-        entry = (slot * 256 + side) * 256 + row
-        own = (behind == 0).astype(jnp.int32)
-        order_ref[1 - own, jnp.where(own == 1, sizes[0], sizes[1])] = entry
+        order_ref[1 - own, jnp.where(own == 1, sizes[0], sizes[1])] = (slot << 16) + (side << 8) + row
         return sizes[0] + own, sizes[1] + 1 - own
 
-    sizes = lax.fori_loop(0, count_ref[0], visit, (jnp.int32(0), jnp.int32(0)))
+    sizes = lax.fori_loop(0, count, visit, (jnp.int32(0), jnp.int32(0)))
     for which in range(2):
         sizes_ref[which] = sizes[which]
         for k in range(UNROLL - 1):
             order_ref[which, sizes[which] + k] = blocks
-
-
-def corner_kernel(place_ref, lead_ref, partner_ref, rest_ref, row_ref, cols_ref, fixed_ref, *, blocks, owners):
+    strip_copy.wait()
+
+    def add(slot, _):
+        row, col = rows_ref[slot], cols_ref[slot]
+        owner, block = col // blocks, lax.rem(col, blocks)
+
+        @pl.when((block == 0) & (owner == 0))
+        def _():
+            lead_ref[pl.ds(row, 1), :] += strips[slot].astype(jnp.float32)[0:1, :]
+
+        @pl.when((block == 0) & (owner > 0))
+        def _():
+            at = pl.ds((owner - 1) * blocks + row, 1)
+            rest_ref[at, :] += strips[slot].astype(jnp.float32)[0:1, :]
+
+        @pl.when(row == 0)
+        def _():
+            tile_copy(slot).wait()
+            column = lax.dot_general(
+                pick, held[slot], (((1,), (1,)), ((), ())), preferred_element_type=jnp.float32
+            )
+            row_ref[pl.ds(col, 1), :] += column[0:1, :]
+
+        return 0
+
+    lax.fori_loop(0, count, add, 0)
+
+
+def corner_kernel(place_ref, lead_ref, partner_ref, rest_ref, row_ref, _, cols_ref, fixed_ref, *, blocks, owners):
     lead, partner = lead_ref[...], partner_ref[...]
     combined = jnp.where(place_ref[0] == 1, partner - lead, partner + lead) * ROOT_HALF
     lines = [combined] + [rest_ref[i * blocks : (i + 1) * blocks, :] for i in range(owners - 1)]
@@ -248,7 +281,7 @@
 
 
 def back_kernel(own_ref, *refs):
-    *arrived, signs_ref, scale_ref, out_ref = refs
+    *arrived, out_ref = refs
     blocks, height, extent = own_ref.shape
     total = own_ref[...]
     for part in arrived:
@@ -256,7 +289,8 @@
     columns = block_inverse([total[b][:, 0:1] for b in range(blocks)])
     lane = lax.broadcasted_iota(jnp.int32, (height, extent), 1)
     fixed = jnp.concatenate([jnp.where(lane == 0, columns[b], total[b]) for b in range(blocks)], axis=0)
-    result = exact_dot(fixed * scale_ref[...], signs_ref[...])
+    signs, scale = haar_parts(extent, True)
+    result = exact_dot(fixed * scale, signs)
     for b in range(blocks):
         out_ref[:, b * extent : (b + 1) * extent] = result[b * height : (b + 1) * height, :]
 
@@ -281,7 +315,6 @@
     row_index, col_index = lax.axis_index("row"), lax.axis_index("col")
     z, x = row_index // owners, row_index % owners
     span, core = col_index // 2, col_index % 2
-    signs, scale = haar_parts(extent)
 
     def moved(value, to):
         pairs = []
@@ -299,6 +332,8 @@
 
     smem = pl.BlockSpec(memory_space=pltpu.SMEM)
     vmem = pl.BlockSpec(memory_space=pltpu.VMEM)
+    hbm = pl.BlockSpec(memory_space=pltpu.HBM)
+    unread = pl.BlockSpec(memory_space=pl.ANY)
 
     def call(kernel, name, out_shape, in_specs, out_specs, limit=16, scratch=(), flops=0, moved_bytes=MIB, **sizes):
         return pl.pallas_call(
@@ -319,23 +354,6 @@
         return jax.ShapeDtypeStruct(dims, jnp.bfloat16)
 
     place = jnp.stack([core, span, x] + [(z - m) % spans for m in range(spans)]).astype(jnp.int32)
-
-    messages = call(
-        front_kernel,
-        "front",
-        [bf16(held * pair + (SIDE_ROWS if q == CHUNKS - 1 else 0), extent) for q in range(CHUNKS)],
-        [smem, vmem, vmem, vmem, vmem],
-        [vmem] * CHUNKS,
-        blocks=blocks,
-        extent=extent,
-    )(place, sources, other_core(sources), jnp.asarray(signs, jnp.bfloat16), jnp.asarray(scale, jnp.float32))
-
-    direct = [
-        moved(messages[q], lambda zz, xx, yy, cc, m=m: (cc * spans + (yy + m) % spans, xx, zz // 2, zz % 2))
-        for m in range(spans)
-        for q in range(CHUNKS)
-    ]
-    swapped = [along_x(piece, j) for j in range(1, owners) for piece in direct]
 
     stack = tiles.reshape(slots, extent, extent)
     rows_flat, cols_flat = tile_row.reshape(-1), tile_col.reshape(-1)
@@ -349,25 +367,57 @@
             jax.ShapeDtypeStruct((2, slots + UNROLL), jnp.int32),
             jax.ShapeDtypeStruct((2,), jnp.int32),
         ],
-        [smem] * 4 + [vmem, pl.BlockSpec(memory_space=pl.ANY)],
+        [smem] * 4 + [hbm],
         [vmem] * 3 + [smem] * 2,
+        limit=48,
+        scratch=[
+            pltpu.VMEM((slots, SIDE_ROWS, extent), jnp.bfloat16),
+            pltpu.VMEM((slots, extent, extent), jnp.bfloat16),
+            pltpu.SemaphoreType.DMA,
+            pltpu.SemaphoreType.DMA((slots,)),
+        ],
         blocks=blocks,
         owners=owners,
-    )(place, rows_flat, cols_flat, tile_count.reshape(1), stack, messages[0])
-
+    )(place, rows_flat, cols_flat, tile_count.reshape(1), stack)
+
+    messages = call(
+        front_kernel,
+        "front",
+        [bf16(held * pair + (SIDE_ROWS if q == CHUNKS - 1 else 0), extent) for q in range(CHUNKS)],
+        [smem, hbm, vmem],
+        [vmem] * CHUNKS,
+        limit=48,
+        scratch=[pltpu.VMEM(sources.shape, jnp.float32), pltpu.SemaphoreType.DMA],
+        blocks=blocks,
+        extent=extent,
+    )(place, sources, other_core(sources))
+
+    direct = [
+        moved(messages[q], lambda zz, xx, yy, cc, m=m: (cc * spans + (yy + m) % spans, xx, zz // 2, zz % 2))
+        for m in range(spans)
+        for q in range(CHUNKS)
+    ]
+    swapped = [along_x(piece, j) for j in range(1, owners) for piece in direct]
+
+    def after(value, *others):
+        return lax.optimization_barrier((value, *others))[0]
+
+
+    lead = after(lead, messages[0])
     for bit in reversed(range(1, n_col.bit_length() - 1)):
         step = 2 ** (bit - 1)
         partner = moved(lead, lambda zz, xx, yy, cc, step=step: (zz, xx, yy ^ step, cc))
         lead = butterfly(lead, partner, col_index, bit)
+    lead = after(lead, direct[0])
     first_cols, first_row = call(
         corner_kernel,
         "corner",
         [f32(owners * blocks, extent)] * 2,
-        [smem] + [vmem] * 4,
+        [smem] + [vmem] * 4 + [unread],
         [vmem] * 2,
         blocks=blocks,
         owners=owners,
-    )(place, lead, other_core(lead), rest, first_row)
+    )(place, lead, other_core(lead), rest, first_row, direct[1])
     behind = [first_row] + [along_x(first_row, j) for j in range(1, owners)]
     by_x = []
     for i in range(owners):
@@ -375,9 +425,11 @@
         for j in range(1, owners):
             line = jnp.where((x - i) % owners == j, behind[j], line)
         by_x.append(line)
+    by_x[0] = after(by_x[0], direct[2], swapped[0])
     for bit in reversed(range((n_row // owners).bit_length() - 1)):
         partner = moved(by_x[0], lambda zz, xx, yy, cc, bit=bit: (zz ^ 2**bit, xx, yy, cc))
         by_x[0] = butterfly(by_x[0], partner, z, bit)
+        by_x[0] = after(by_x[0], direct[-1], *swapped[1 : 2 if bit else 3])
     by_x = block_inverse(by_x)
     first_row = by_x[0]
     for i in range(1, owners):
@@ -431,9 +483,7 @@
     arrived = [
         moved(value, lambda zz, xx, yy, cc, j=j: (zz, xx, (yy + j) % spans, cc)) for j, value in enumerate(outgoing, 1)
     ]
-    return call(back_kernel, "back", f32(*sources.shape), [vmem] * (spans + 2), vmem)(
-        own, *arrived, jnp.asarray(signs.T, jnp.bfloat16), jnp.asarray(scale, jnp.float32)
-    )
+    return call(back_kernel, "back", f32(*sources.shape), [vmem] * spans, vmem)(own, *arrived)
 
 
 def solution(mesh):

time: 61 us -> 62.2 us (1.020)
  local copies, waits for them, and re-layouts: 9.51 us -> 4.85 us
  waiting for transfers between devices: 14.8 us -> 18.3 us
  starting transfers between devices: 25.5 us -> 28.4 us
    unnamed x22 -> x12, local copies, waits for them, and re-layouts: 9.42 us -> 4.76 us
    ppermute x16, waiting for transfers between devices: 14.8 us -> 18.3 us  [moved(): return lax.ppermute(value, ('row', 'col'), pairs)]
    ppermute x16, starting transfers between devices: 25.5 us -> 28.4 us  [moved(): return lax.ppermute(value, ('row', 'col'), pairs)]
  transfers between devices with their start and end apart: 16 -> 16, of which waited for: 8 -> 7; matrix products, arithmetic and copies ran while one was open for 0% -> 0% of each run, Pallas kernels for 3% -> 7%
where the time goes in v3:
time: 62.2 us; the launch traced here: 62.1 us
  starting transfers between devices  28.4 us (46%)
  waiting for transfers between devices  18.3 us (29%)
  Pallas kernels  9.67 us (16%)
  local copies, waits for them, and re-layouts  4.85 us (8%)
  between operations  0.82 us (1%)
    ppermute x16, starting transfers between devices, moved(): return lax.ppermute(value, ('row', 'col'), pairs)  28.4 us
    ppermute x16, waiting for transfers between devices, moved(): return lax.ppermute(value, ('row', 'col'), pairs)  18.3 us
    unnamed x12, local copies, waits for them, and re-layouts  4.76 us
    pallas_call x1, Pallas kernels, local(): call(edge_kernel, 'edges', [f32(blocks, extent), f32((owners - 1) * block...  2.68 us
    pallas_call x1, Pallas kernels, local(): call(far_kernel, 'far', [f32(*shape)] * 2, [smem] * 3 + [vmem] * (4 + len...  2.11 us
    pallas_call x1, Pallas kernels, local(): call(near_kernel, 'near', f32(blocks + 1, *every), [smem] * 3 + [vmem] *...  1.44 us
  transfers between devices with their start and end apart: 16, of which 7 were waited for; matrix products, arithmetic and copies ran while one was open for 0% of the time, Pallas kernels for 7%

profile of v3, /device:TPU:0, one launch (start us, length us, event | category | flops | bytes accessed | tf_op | source)
XLA Modules:
  0.0 62.1 jit_solution(5790624238169496381)
XLA Ops:
  1.2 0.7 %copy-done.2 = s32[1,1,48]{2,1,0:T(1,128)S(1)} copy-done((s32[1,1,48]{2,1,0:T(1,128)S(1)}, s32[1,1,48]{2,1,0:T(1,128)}, u32[]{:S(2)}) %copy-start.2) | copy-done | bytes 216
  2.5 2.7 %edges.1 = (f32[8,256]{1,0:T(8,128)S(1)}, f32[8,256]{1,0:T(8,128)S(1)}, f32[16,256]{1,0:T(8,128)S(1)}, s32[2,52]{1,0:T(2,128)S(1)}, s32[2]{0:T(128)S(1)}) custom-call(s32[5]{0:T(128)S(1)} %stack.23.place_ref.core_ref, s32[48]{0:T(128)S(1)} %bitcast.15, s32[48]{0:T(128)S(1)} %bitcast.16, s32[1]{0:T(128)} %bitcast.9.count_ref, bf16[48,256,256]{2,1,0:T(8,128)(2,1)} %bitcast.10), custom_call_target="tpu_custom_call" | custom-call | bytes 1048576 | tf_op jit(solution)/shard_map/edges/pallas_call | solution.py:360
  5.2 1.2 %front.1 = (bf16[256,256]{1,0:T(8,128)(2,1)S(1)}, bf16[272,256]{1,0:T(8,128)(2,1)S(1)}) custom-call(s32[5]{0:T(128)S(1)} %stack.23.place_ref.core_ref, f32[32,2048]{1,0:T(8,128)S(1)} %copy-done.1, f32[32,2048]{1,0:T(8,128)S(1)} %collective-permute-done.other_ref), custom_call_target="tpu_custom_call" | custom-call | bytes 1048576 | tf_op jit(solution)/shard_map/front/pallas_call | solution.py:383
  6.4 4.0 %collective-permute-start.5 = (f32[8,256]{1,0:T(8,128)S(1)}, f32[8,256]{1,0:T(8,128)S(1)}, u32[]{:S(2)}, u32[]{:S(2)}) collective-permute-start(f32[8,256]{1,0:T(8,128)S(1)} %get-tuple-element.28), channel_id=1, source_target_pairs={{0,2},{1,3},{2,0},{3,1},{4,6},{5,7},{6,4},{7,5},{8,10},{9,11},{10,... | collective-permute-start | bytes 24584 | tf_op jit(solution)/shard_map/ppermute | solution.py:325
  10.4 0.7 %collective-permute-start.1 = (bf16[256,256]{1,0:T(8,128)(2,1)S(1)}, bf16[256,256]{1,0:T(8,128)(2,1)S(1)}, u32[]{:S(2)}, u32[]{:S(2)}) collective-permute-start(bf16[256,256]{1,0:T(8,128)(2,1)S(1)} %get-tuple-element.25), channel_id=1, source_target_pairs={{0,0},{1,16},{2,8},{3,24},{4,4},{5,20},{6,12},{7,28},{8,1},{9,17},... | collective-permute-start | bytes 393224 | tf_op jit(solution)/shard_map/ppermute | solution.py:325
  11.1 0.7 %collective-permute-start.2 = (bf16[272,256]{1,0:T(8,128)(2,1)S(1)}, bf16[272,256]{1,0:T(8,128)(2,1)S(1)}, u32[]{:S(2)}, u32[]{:S(2)}) collective-permute-start(bf16[272,256]{1,0:T(8,128)(2,1)S(1)} %get-tuple-element.26), channel_id=1, source_target_pairs={{0,0},{1,16},{2,8},{3,24},{4,4},{5,20},{6,12},{7,28},{8,1},{9,17},... | collective-permute-start | bytes 417800 | tf_op jit(solution)/shard_map/ppermute | solution.py:325
  12.1 4.8 %collective-permute-start.6 = (f32[8,256]{1,0:T(8,128)S(1)}, f32[8,256]{1,0:T(8,128)S(1)}, u32[]{:S(2)}, u32[]{:S(2)}) collective-permute-start(f32[8,256]{1,0:T(8,128)S(1)} %multiply_select_fusion.2.lead_ref), channel_id=1, source_target_pairs={{0,1},{1,0},{2,3},{3,2},{4,5},{5,4},{6,7},{7,6},{8,9},{9,8},{10,11... | collective-permute-start | bytes 24584 | tf_op jit(solution)/shard_map/ppermute | solution.py:325
  16.9 0.8 %collective-permute-done.6.partner_ref = f32[8,256]{1,0:T(8,128)S(1)} collective-permute-done((f32[8,256]{1,0:T(8,128)S(1)}, f32[8,256]{1,0:T(8,128)S(1)}, u32[]{:S(2)}, u32[]{:S(2)}) %collective-permute-start.6) | collective-permute-done | bytes 8224 | tf_op jit(solution)/shard_map/ppermute | solution.py:325
  18.3 2.0 %collective-permute-start.7 = (f32[16,256]{1,0:T(8,128)S(1)}, f32[16,256]{1,0:T(8,128)S(1)}, u32[]{:S(2)}, u32[]{:S(2)}) collective-permute-start(f32[16,256]{1,0:T(8,128)S(1)} %get-tuple-element.33), channel_id=1, source_target_pairs={{0,4},{1,5},{2,6},{3,7},{4,0},{5,1},{6,2},{7,3},{8,12},{9,13},{10,... | collective-permute-start | bytes 49160 | tf_op jit(solution)/shard_map/ppermute | solution.py:325
  20.3 4.0 %collective-permute-start.3 = (bf16[256,256]{1,0:T(8,128)(2,1)S(1)}, bf16[256,256]{1,0:T(8,128)(2,1)S(1)}, u32[]{:S(2)}, u32[]{:S(2)}) collective-permute-start(bf16[256,256]{1,0:T(8,128)(2,1)S(1)} %get-tuple-element.25), channel_id=1, source_target_pairs={{0,8},{1,24},{2,0},{3,16},{4,12},{5,28},{6,4},{7,20},{8,9},{9,25},... | collective-permute-start | bytes 393224 | tf_op jit(solution)/shard_map/ppermute | solution.py:325
  24.3 0.7 %collective-permute-start.8 = (bf16[256,256]{1,0:T(8,128)(2,1)S(1)}, bf16[256,256]{1,0:T(8,128)(2,1)S(1)}, u32[]{:S(2)}, u32[]{:S(2)}) collective-permute-start(bf16[256,256]{1,0:T(8,128)(2,1)S(1)} %collective-permute-done.1.refs_0_), channel_id=1, source_target_pairs={{0,4},{1,5},{2,6},{3,7},{4,0},{5,1},{6,2},{7,3},{8,12},{9,13},{10,... | collective-permute-start | bytes 393224 | tf_op jit(solution)/shard_map/ppermute | solution.py:325
  25.1 3.0 %collective-permute-done.3.refs_2_ = bf16[256,256]{1,0:T(8,128)(2,1)S(1)} collective-permute-done((bf16[256,256]{1,0:T(8,128)(2,1)S(1)}, bf16[256,256]{1,0:T(8,128)(2,1)S(1)}, u32[]{:S(2)}, u32[]{:S(2)}) %collective-permute-start.3) | collective-permute-done | bytes 131104 | tf_op jit(solution)/shard_map/ppermute | solution.py:325
  28.1 1.2 %collective-permute-done.8.refs_4_ = bf16[256,256]{1,0:T(8,128)(2,1)S(1)} collective-permute-done((bf16[256,256]{1,0:T(8,128)(2,1)S(1)}, bf16[256,256]{1,0:T(8,128)(2,1)S(1)}, u32[]{:S(2)}, u32[]{:S(2)}) %collective-permute-start.8) | collective-permute-done | bytes 131104 | tf_op jit(solution)/shard_map/ppermute | solution.py:325
  29.3 6.7 %collective-permute-start.9 = (f32[16,256]{1,0:T(8,128)S(1)}, f32[16,256]{1,0:T(8,128)S(1)}, u32[]{:S(2)}, u32[]{:S(2)}) collective-permute-start(f32[16,256]{1,0:T(8,128)S(1)} %broadcast_select_fusion), channel_id=1, source_target_pairs={{0,16},{1,17},{2,18},{3,19},{4,20},{5,21},{6,22},{7,23},{8,24},{9,... | collective-permute-start | bytes 49160 | tf_op jit(solution)/shard_map/ppermute | solution.py:325
  36.0 2.0 %collective-permute-start.10 = (bf16[272,256]{1,0:T(8,128)(2,1)S(1)}, bf16[272,256]{1,0:T(8,128)(2,1)S(1)}, u32[]{:S(2)}, u32[]{:S(2)}) collective-permute-start(bf16[272,256]{1,0:T(8,128)(2,1)S(1)} %collective-permute-done.2.refs_1_._), channel_id=1, source_target_pairs={{0,4},{1,5},{2,6},{3,7},{4,0},{5,1},{6,2},{7,3},{8,12},{9,13},{10,... | collective-permute-start | bytes 417800 | tf_op jit(solution)/shard_map/ppermute | solution.py:325
  38.1 7.2 %collective-permute-done.10.refs_5_ = bf16[272,256]{1,0:T(8,128)(2,1)S(1)} collective-permute-done((bf16[272,256]{1,0:T(8,128)(2,1)S(1)}, bf16[272,256]{1,0:T(8,128)(2,1)S(1)}, u32[]{:S(2)}, u32[]{:S(2)}) %collective-permute-start.10) | collective-permute-done | bytes 139296 | tf_op jit(solution)/shard_map/ppermute | solution.py:325
  45.3 2.8 %copy-done = bf16[1,1,48,256,256]{4,3,2,1,0:T(8,128)(2,1)S(1)} copy-done((bf16[1,1,48,256,256]{4,3,2,1,0:T(8,128)(2,1)S(1)}, bf16[1,1,48,256,256]{4,3,2,1,0:T(8,128)(2,1)}, u32[]{:S(2)}) %copy-start) | copy-done | bytes 6291480
  48.1 1.4 %near.1.near_ref = f32[9,128,256]{2,1,0:T(8,128)S(1)} custom-call(s32[5]{0:T(128)S(1)} %stack.23.place_ref.core_ref, s32[2,52]{1,0:T(2,128)S(1)} %get-tuple-element.23.order_ref, s32[2]{0:T(128)S(1)} %get-tuple-element.24.sizes_ref, bf16[48,256,256]{2,1,0:T(8,128)(2,1)S(1)} %bitcast.11, bf16[256,256]{1,0:T(8,128)(2,1)S(1)} %collective-permute-done.1.refs_0_, ...), custom_call_target="tpu_custom_call" | custom-call | flops 402653184 | bytes 6291456 | tf_op jit(solution)/shard_map/near/pallas_call | solution.py:440
  49.6 0.7 %slice-done.1 = s8[4194304]{0:T(1024)(128)(4,1)S(1)} async-done(((s8[6291456]{0:T(1024)(128)(4,1)}), s8[4194304]{0:T(1024)(128)(4,1)S(1)}, s32[]{:S(2)}) %slice-start.1) | async-done | bytes 4194328
  50.3 2.1 %far.1 = (f32[2,8,32,256]{3,2,1,0:T(8,128)S(1)}, f32[2,8,32,256]{3,2,1,0:T(8,128)S(1)}) custom-call(s32[5]{0:T(128)S(1)} %stack.23.place_ref.core_ref, s32[2,52]{1,0:T(2,128)S(1)} %get-tuple-element.23.order_ref, s32[2]{0:T(128)S(1)} %get-tuple-element.24.sizes_ref, bf16[48,256,256]{2,1,0:T(8,128)(2,1)S(1)} %bitcast.14, f32[9,128,256]{2,1,0:T(8,128)S(1)} %near.1.near_ref, ...), custom_call_target="tpu_custom_call" | custom-call | flops 805306368 | bytes 6291456 | tf_op jit(solution)/shard_map/far/pallas_call | solution.py:456
  52.5 1.9 %collective-permute-done.14.arrived_ref = f32[2,8,32,256]{3,2,1,0:T(8,128)S(1)} collective-permute-done((f32[2,8,32,256]{3,2,1,0:T(8,128)S(1)}, f32[2,8,32,256]{3,2,1,0:T(8,128)S(1)}, u32[]{:S(2)}, u32[]{:S(2)}) %collective-permute-start.14) | collective-permute-done | bytes 524320 | tf_op jit(solution)/shard_map/ppermute | solution.py:325
  55.0 2.2 %collective-permute-start.15 = (bf16[8,32,256]{2,1,0:T(8,128)(2,1)S(1)}, bf16[8,32,256]{2,1,0:T(8,128)(2,1)S(1)}, u32[]{:S(2)}, u32[]{:S(2)}) collective-permute-start(bf16[8,32,256]{2,1,0:T(8,128)(2,1)S(1)} %get-tuple-element.40), channel_id=1, source_target_pairs={{0,2},{1,3},{2,0},{3,1},{4,6},{5,7},{6,4},{7,5},{8,10},{9,11},{10,... | collective-permute-start | bytes 393224 | tf_op jit(solution)/shard_map/ppermute | solution.py:325
  57.2 3.8 %collective-permute-done.15.refs_0_ = bf16[8,32,256]{2,1,0:T(8,128)(2,1)S(1)} collective-permute-done((bf16[8,32,256]{2,1,0:T(8,128)(2,1)S(1)}, bf16[8,32,256]{2,1,0:T(8,128)(2,1)S(1)}, u32[]{:S(2)}, u32[]{:S(2)}) %collective-permute-start.15) | collective-permute-done | bytes 131104 | tf_op jit(solution)/shard_map/ppermute | solution.py:325
  61.0 1.1 %back.1 = f32[32,2048]{1,0:T(8,128)} custom-call(f32[8,32,256]{2,1,0:T(8,128)S(1)} %get-tuple-element.39.own_ref, bf16[8,32,256]{2,1,0:T(8,128)(2,1)S(1)} %collective-permute-done.15.refs_0_), custom_call_target="tpu_custom_call" | custom-call | bytes 1048576 | tf_op jit(solution)/shard_map/back/pallas_call | solution.py:486
  (34 shorter events, 2.9 us)
Async XLA Ops:
  0.0 5.2 %copy-start.1 = (f32[32,2048]{1,0:T(8,128)S(1)}, f32[32,2048]{1,0:T(8,128)}, u32[]{:S(2)}) copy-start(f32[32,2048]{1,0:T(8,128)} %sources_ref.1) | copy-start | bytes 786436
  0.0 5.2 %collective-permute-start = (f32[32,2048]{1,0:T(8,128)}, f32[32,2048]{1,0:T(8,128)S(1)}, u32[]{:S(2)}, u32[]{:S(2)}) collective-permute-start(f32[32,2048]{1,0:T(8,128)} %sources_ref.1), channel_id=1, source_target_pairs={{0,1},{1,0},{2,3},{3,2},{4,5},{5,4},{6,7},{7,6},{8,9},{9,8},{10,11... | collective-permute-start | bytes 786440 | tf_op jit(solution)/shard_map/ppermute | solution.py:325
  1.2 0.7 %copy-start.2 = (s32[1,1,48]{2,1,0:T(1,128)S(1)}, s32[1,1,48]{2,1,0:T(1,128)}, u32[]{:S(2)}) copy-start(s32[1,1,48]{2,1,0:T(1,128)} %param.7) | copy-start | bytes 580
  1.9 0.7 %copy-start.3 = (s32[1,1,48]{2,1,0:T(1,128)S(1)}, s32[1,1,48]{2,1,0:T(1,128)}, u32[]{:S(2)}) copy-start(s32[1,1,48]{2,1,0:T(1,128)} %param.8) | copy-start | bytes 580
  2.5 47.1 %slice-start = ((s8[6291456]{0:T(1024)(128)(4,1)}), s8[2097152]{0:T(1024)(128)(4,1)S(1)}, s32[]{:S(2)}) async-start(s8[6291456]{0:T(1024)(128)(4,1)} %bitcast.12), calls=%async_computation | async-start | bytes 4194304
  6.4 5.7 %collective-permute-start.5 = (f32[8,256]{1,0:T(8,128)S(1)}, f32[8,256]{1,0:T(8,128)S(1)}, u32[]{:S(2)}, u32[]{:S(2)}) collective-permute-start(f32[8,256]{1,0:T(8,128)S(1)} %get-tuple-element.28), channel_id=1, source_target_pairs={{0,2},{1,3},{2,0},{3,1},{4,6},{5,7},{6,4},{7,5},{8,10},{9,11},{10,... | collective-permute-start | bytes 24584 | tf_op jit(solution)/shard_map/ppermute | solution.py:325
  10.4 1.6 %collective-permute-start.1 = (bf16[256,256]{1,0:T(8,128)(2,1)S(1)}, bf16[256,256]{1,0:T(8,128)(2,1)S(1)}, u32[]{:S(2)}, u32[]{:S(2)}) collective-permute-start(bf16[256,256]{1,0:T(8,128)(2,1)S(1)} %get-tuple-element.25), channel_id=1, source_target_pairs={{0,0},{1,16},{2,8},{3,24},{4,4},{5,20},{6,12},{7,28},{8,1},{9,17},... | collective-permute-start | bytes 393224 | tf_op jit(solution)/shard_map/ppermute | solution.py:325
  11.1 6.6 %collective-permute-start.2 = (bf16[272,256]{1,0:T(8,128)(2,1)S(1)}, bf16[272,256]{1,0:T(8,128)(2,1)S(1)}, u32[]{:S(2)}, u32[]{:S(2)}) collective-permute-start(bf16[272,256]{1,0:T(8,128)(2,1)S(1)} %get-tuple-element.26), channel_id=1, source_target_pairs={{0,0},{1,16},{2,8},{3,24},{4,4},{5,20},{6,12},{7,28},{8,1},{9,17},... | collective-permute-start | bytes 417800 | tf_op jit(solution)/shard_map/ppermute | solution.py:325
  12.1 5.6 %collective-permute-start.6 = (f32[8,256]{1,0:T(8,128)S(1)}, f32[8,256]{1,0:T(8,128)S(1)}, u32[]{:S(2)}, u32[]{:S(2)}) collective-permute-start(f32[8,256]{1,0:T(8,128)S(1)} %multiply_select_fusion.2.lead_ref), channel_id=1, source_target_pairs={{0,1},{1,0},{2,3},{3,2},{4,5},{5,4},{6,7},{7,6},{8,9},{9,8},{10,11... | collective-permute-start | bytes 24584 | tf_op jit(solution)/shard_map/ppermute | solution.py:325
  18.3 6.7 %collective-permute-start.7 = (f32[16,256]{1,0:T(8,128)S(1)}, f32[16,256]{1,0:T(8,128)S(1)}, u32[]{:S(2)}, u32[]{:S(2)}) collective-permute-start(f32[16,256]{1,0:T(8,128)S(1)} %get-tuple-element.33), channel_id=1, source_target_pairs={{0,4},{1,5},{2,6},{3,7},{4,0},{5,1},{6,2},{7,3},{8,12},{9,13},{10,... | collective-permute-start | bytes 49160 | tf_op jit(solution)/shard_map/ppermute | solution.py:325
  20.3 7.8 %collective-permute-start.3 = (bf16[256,256]{1,0:T(8,128)(2,1)S(1)}, bf16[256,256]{1,0:T(8,128)(2,1)S(1)}, u32[]{:S(2)}, u32[]{:S(2)}) collective-permute-start(bf16[256,256]{1,0:T(8,128)(2,1)S(1)} %get-tuple-element.25), channel_id=1, source_target_pairs={{0,8},{1,24},{2,0},{3,16},{4,12},{5,28},{6,4},{7,20},{8,9},{9,25},... | collective-permute-start | bytes 393224 | tf_op jit(solution)/shard_map/ppermute | solution.py:325
  24.3 13.7 %collective-permute-start.4 = (bf16[272,256]{1,0:T(8,128)(2,1)S(1)}, bf16[272,256]{1,0:T(8,128)(2,1)S(1)}, u32[]{:S(2)}, u32[]{:S(2)}) collective-permute-start(bf16[272,256]{1,0:T(8,128)(2,1)S(1)} %get-tuple-element.26), channel_id=1, source_target_pairs={{0,8},{1,24},{2,0},{3,16},{4,12},{5,28},{6,4},{7,20},{8,9},{9,25},... | collective-permute-start | bytes 417800 | tf_op jit(solution)/shard_map/ppermute | solution.py:325
  24.3 5.0 %collective-permute-start.8 = (bf16[256,256]{1,0:T(8,128)(2,1)S(1)}, bf16[256,256]{1,0:T(8,128)(2,1)S(1)}, u32[]{:S(2)}, u32[]{:S(2)}) collective-permute-start(bf16[256,256]{1,0:T(8,128)(2,1)S(1)} %collective-permute-done.1.refs_0_), channel_id=1, source_target_pairs={{0,4},{1,5},{2,6},{3,7},{4,0},{5,1},{6,2},{7,3},{8,12},{9,13},{10,... | collective-permute-start | bytes 393224 | tf_op jit(solution)/shard_map/ppermute | solution.py:325
  29.3 8.8 %collective-permute-start.9 = (f32[16,256]{1,0:T(8,128)S(1)}, f32[16,256]{1,0:T(8,128)S(1)}, u32[]{:S(2)}, u32[]{:S(2)}) collective-permute-start(f32[16,256]{1,0:T(8,128)S(1)} %broadcast_select_fusion), channel_id=1, source_target_pairs={{0,16},{1,17},{2,18},{3,19},{4,20},{5,21},{6,22},{7,23},{8,24},{9,... | collective-permute-start | bytes 49160 | tf_op jit(solution)/shard_map/ppermute | solution.py:325
  36.0 13.6 %collective-permute-start.12 = (bf16[256,256]{1,0:T(8,128)(2,1)S(1)}, bf16[256,256]{1,0:T(8,128)(2,1)S(1)}, u32[]{:S(2)}, u32[]{:S(2)}) collective-permute-start(bf16[256,256]{1,0:T(8,128)(2,1)S(1)} %collective-permute-done.3.refs_2_), channel_id=1, source_target_pairs={{0,4},{1,5},{2,6},{3,7},{4,0},{5,1},{6,2},{7,3},{8,12},{9,13},{10,... | collective-permute-start | bytes 393224 | tf_op jit(solution)/shard_map/ppermute | solution.py:325
  36.0 9.3 %collective-permute-start.10 = (bf16[272,256]{1,0:T(8,128)(2,1)S(1)}, bf16[272,256]{1,0:T(8,128)(2,1)S(1)}, u32[]{:S(2)}, u32[]{:S(2)}) collective-permute-start(bf16[272,256]{1,0:T(8,128)(2,1)S(1)} %collective-permute-done.2.refs_1_._), channel_id=1, source_target_pairs={{0,4},{1,5},{2,6},{3,7},{4,0},{5,1},{6,2},{7,3},{8,12},{9,13},{10,... | collective-permute-start | bytes 417800 | tf_op jit(solution)/shard_map/ppermute | solution.py:325
  38.0 11.6 %collective-permute-start.13 = (bf16[272,256]{1,0:T(8,128)(2,1)S(1)}, bf16[272,256]{1,0:T(8,128)(2,1)S(1)}, u32[]{:S(2)}, u32[]{:S(2)}) collective-permute-start(bf16[272,256]{1,0:T(8,128)(2,1)S(1)} %collective-permute-done.4.refs_3_), channel_id=1, source_target_pairs={{0,4},{1,5},{2,6},{3,7},{4,0},{5,1},{6,2},{7,3},{8,12},{9,13},{10,... | collective-permute-start | bytes 417800 | tf_op jit(solution)/shard_map/ppermute | solution.py:325
  45.3 4.2 %collective-permute-start.11 = (f32[16,256]{1,0:T(8,128)S(1)}, f32[16,256]{1,0:T(8,128)S(1)}, u32[]{:S(2)}, u32[]{:S(2)}) collective-permute-start(f32[16,256]{1,0:T(8,128)S(1)} %multiply_select_fusion.1), channel_id=1, source_target_pairs={{0,8},{1,9},{2,10},{3,11},{4,12},{5,13},{6,14},{7,15},{8,0},{9,1},... | collective-permute-start | bytes 49160 | tf_op jit(solution)/shard_map/ppermute | solution.py:325
  45.3 2.8 %copy-start = (bf16[1,1,48,256,256]{4,3,2,1,0:T(8,128)(2,1)S(1)}, bf16[1,1,48,256,256]{4,3,2,1,0:T(8,128)(2,1)}, u32[]{:S(2)}) copy-start(bf16[1,1,48,256,256]{4,3,2,1,0:T(8,128)(2,1)} %param.6) | copy-start | bytes 18874372
  48.1 2.2 %slice-start.1 = ((s8[6291456]{0:T(1024)(128)(4,1)}), s8[4194304]{0:T(1024)(128)(4,1)S(1)}, s32[]{:S(2)}) async-start(s8[6291456]{0:T(1024)(128)(4,1)} %bitcast.12), calls=%async_computation.1 | async-start | bytes 8388608
  52.4 2.0 %collective-permute-start.14 = (f32[2,8,32,256]{3,2,1,0:T(8,128)S(1)}, f32[2,8,32,256]{3,2,1,0:T(8,128)S(1)}, u32[]{:S(2)}, u32[]{:S(2)}) collective-permute-start(f32[2,8,32,256]{3,2,1,0:T(8,128)S(1)} %get-tuple-element.38), channel_id=1, source_target_pairs={{0,1},{1,0},{2,3},{3,2},{4,5},{5,4},{6,7},{7,6},{8,9},{9,8},{10,11... | collective-permute-start | bytes 1572872 | tf_op jit(solution)/shard_map/ppermute | solution.py:325
  55.0 6.0 %collective-permute-start.15 = (bf16[8,32,256]{2,1,0:T(8,128)(2,1)S(1)}, bf16[8,32,256]{2,1,0:T(8,128)(2,1)S(1)}, u32[]{:S(2)}, u32[]{:S(2)}) collective-permute-start(bf16[8,32,256]{2,1,0:T(8,128)(2,1)S(1)} %get-tuple-element.40), channel_id=1, source_target_pairs={{0,2},{1,3},{2,0},{3,1},{4,6},{5,7},{6,4},{7,5},{8,10},{9,11},{10,... | collective-permute-start | bytes 393224 | tf_op jit(solution)/shard_map/ppermute | solution.py:325
